TPU v7x, 512 devices: a whole 4x4x16 slice. The times are simulated.
512 devices in a mesh: grp: 64 (over z, x), mem: 8 (over y, core).
Axes of the slice: x: 4, y: 4, z: 16, core: 2. Of those that a mesh axis runs over, the one named last changes fastest.
Arguments:
- embeddings: bfloat16 [64, 32, 64, 768], P('grp', 'mem'), may hold values from -30 to 30
- counts: int32 [64, 64], replicated, may hold values from 0 to 32, as said below
Outputs:
- nearest: float32 [64, 32, 64], P('grp', 'mem')
Inputs may be any that keep to these rules, and one draw needn't show every extreme that they name: counts[s, c] slots of source group s for cluster c are filled, the first ones; some entry equals 32 and some equals 0.
All inputs are finite; a program needn't handle non-finite values.
Results may differ from a plain program's by a relative error of at most 0.00067.
Values may be sent and summed in bfloat16 or wider, within the bound.
No kernel may reach another device: no remote copies, remote signals or barrier semaphores. Data moves between devices by JAX's collectives and lax.ppermute only.
A program may use at most 64 MiB of HBM per device.

v0:
```python
import jax
import jax.numpy as jnp
from jax import lax
from jax.sharding import PartitionSpec as P

EPS = 1e-06


def on_device(embeddings, counts):
    cluster = lax.axis_index("grp")
    member = lax.axis_index("mem")
    slot_dev = embeddings.shape[1]
    groups = embeddings.shape[2]
    width = embeddings.shape[3]
    local = embeddings.reshape(slot_dev, groups, width)
    values = local.astype(jnp.float32)
    units = (values * lax.rsqrt(jnp.sum(values * values, axis=-1, keepdims=True) + EPS)).astype(
        jnp.bfloat16
    )
    owned = lax.all_to_all(units, "grp", split_axis=1, concat_axis=1, tiled=True)
    nrows = slot_dev * groups
    rows = owned.reshape(nrows, width)
    own_start = member * nrows
    own_pos = own_start + jnp.arange(nrows, dtype=jnp.int32)
    sizes = lax.dynamic_index_in_dim(counts, cluster, 1, keepdims=False)
    source_ids = jnp.arange(groups, dtype=jnp.int32)
    initial = jnp.full((nrows,), -1.0, jnp.float32)
    piece = lax.all_gather(rows, "mem", axis=0, tiled=True)
    count = piece.shape[0]
    pos = jnp.arange(count, dtype=jnp.int32)
    slot_of = pos // groups
    source_of = pos % groups
    size_of = jnp.sum(
        jnp.where(source_of[:, None] == source_ids[None, :], sizes[None, :], 0), axis=1
    )
    filled = (slot_of < size_of) & (pos >= 0)
    scores = jnp.dot(rows, piece.T, preferred_element_type=jnp.float32)
    allowed = filled[None, :] & (pos[None, :] < own_pos[:, None])
    best = jnp.maximum(initial, jnp.max(jnp.where(allowed, scores, jnp.float32(-1.0)), axis=1))
    back = lax.all_to_all(
        best.reshape(slot_dev, groups), "grp", split_axis=1, concat_axis=1, tiled=True
    )
    return back.reshape(1, slot_dev, groups)


def solution(mesh):
    return jax.shard_map(
        on_device,
        mesh=mesh,
        in_specs=(P("grp", "mem", None, None), P()),
        out_specs=P("grp", "mem", None),
        check_vma=False,
    )
```

profile of v0, /device:TPU:24, one launch (start us, length us, event | category | flops | bytes accessed | tf_op | source)
XLA Modules:
  0.0 122.5 jit_solution(1794902101952908260)
XLA Ops:
  6.5 0.0 copy-start
  6.5 0.0 all-gather.2.cloned.1.call-start
  6.5 1.4 %fusion.2 = f32[4,64]{0,1:T(8,128)S(1)} fusion(bf16[1,4,64,768]{3,2,1,0:T(8,128)(2,1)} %param.2), kind=kLoop, calls=%fused_computation.6 | loop fusion | flops 589568 | bytes 394240 | tf_op jit(solution)/shard_map/reduce_sum | solution.py:17
  7.9 1.3 %fusion.3 = bf16[4,64,768]{2,0,1:T(4,128)(2,1)S(1)} fusion(f32[4,64]{0,1:T(8,128)S(1)} %add_rsqrt_fusion, bf16[1,4,64,768]{3,2,1,0:T(8,128)(2,1)} %param.2), kind=kLoop, calls=%fused_computation.7 | loop fusion | flops 589824 | bytes 787456 | tf_op jit(solution)/shard_map/convert_element_type | solution.py:17
  9.3 45.7 %all_to_all.11 = bf16[4,64,768]{2,0,1:T(4,128)(2,1)S(1)} all-to-all(bf16[4,64,768]{2,0,1:T(4,128)(2,1)S(1)} %fusion.3), channel_id=1, replica_groups=mesh['grp'=64,'mem'=8] {'grp'}, dimensions={1} | all-to-all | bytes 786432 | tf_op jit(solution)/shard_map/all_to_all | solution.py:20
  54.9 0.8 copy.10
  55.7 0.0 all-gather.2.cloned.1.call-update
  55.8 0.0 copy-done
  55.8 0.2 dynamic-slice_reduce_fusion
  56.0 0.2 select_reduce_fusion
  56.2 25.4 %all-gather.2.cloned.1.call-done = bf16[2048,768]{1,0:T(8,128)(2,1)} async-done(((bf16[256,768]{1,0:T(8,128)(2,1)}), bf16[2048,768]{1,0:T(8,128)(2,1)}) %all-gather.2.cloned.1.call-update) | async-done | bytes 3145744 | tf_op jit(solution)/shard_map/all_gather | solution.py:28
  81.6 3.2 %fusion.1 = f32[256]{0:T(256)S(1)} fusion(bf16[256,768]{1,0:T(8,128)(2,1)} %bitcast.9, bf16[2048,768]{1,0:T(8,128)(2,1)} %all-gather.2.cloned.1.call-done, s32[256]{0:T(256)S(1)} %iota_add_fusion, pred[2048]{0:T(1024)(128)(4,1)S(1)} %fusion.10), kind=kOutput, calls=%fused_computation.3 | convolution fusion | flops 807403264 | bytes 3543040 | tf_op jit(solution)/shard_map/dot_general | solution.py:37
  84.8 0.1 max_broadcast_in_dim.15
  84.9 0.1 copy.11
  85.0 30.0 %all_to_all.12 = f32[4,64,1]{0,2,1:T(1,128)S(1)} all-to-all(f32[4,64,1]{0,2,1:T(1,128)S(1)} %copy.11), channel_id=1, replica_groups=mesh['grp'=64,'mem'=8] {'grp'}, dimensions={1} | all-to-all | bytes 2048 | tf_op jit(solution)/shard_map/all_to_all | solution.py:40
  115.0 0.7 copy.12
  (5 shorter events, 0.0 us)
Async XLA Ops:
  6.5 49.2 %copy-start = (s32[64,64]{1,0:T(8,128)S(1)}, s32[64,64]{1,0:T(8,128)}, u32[]{:S(2)}) copy-start(s32[64,64]{1,0:T(8,128)} %param.3) | copy-start | bytes 49156
  6.5 75.0 %all-gather.2.cloned.1.call-start = ((), (), s32[]{:S(2)}) async-start(), calls=%async_computation.2 | async-start | bytes 3538944 | tf_op jit(solution)/shard_map/all_gather | solution.py:28
Sparse Core Ops, SparseCore 0:
  55.9 25.6 all-gather.1
where the time goes:
time: 124 us; the launch traced here: 123 us
  blocking collectives  75.7 us (61%)
  waiting for transfers between devices  25.4 us (20%)
  between operations  13.4 us (11%)
  matrix products  3.23 us (3%)
  other arithmetic  2.9 us (2%)
  local copies, waits for them, and re-layouts  1.79 us (1%)
    all_to_all x1, blocking collectives, on_device(): lax.all_to_all(units, 'grp', split_axis=1, concat_axis=1, tiled=True)  45.7 us
    all_to_all x1, blocking collectives, on_device(): lax.all_to_all(best.reshape(slot_dev, groups), 'grp', split_axis=1, conca...  30 us
    all_gather x1, waiting for transfers between devices, on_device(): piece = lax.all_gather(rows, 'mem', axis=0, tiled=True)  25.4 us
    dot_general x1, matrix products, on_device(): scores = jnp.dot(rows, piece.T, preferred_element_type=jnp.float32)  3.23 us
  transfers between devices with their start and end apart: 1, of which 1 were waited for; matrix products, arithmetic and copies ran while one was open for 0% of the time, Pallas kernels for 0%

commit v1 on v0

v1 whole, which is shorter than its diff:
```python
import jax
import jax.numpy as jnp
from jax import lax
from jax.experimental import pallas as pl
from jax.experimental.pallas import tpu as pltpu
from jax.sharding import PartitionSpec as P

EPS = 1e-06
FAR = 1 << 20
CORES = 2


def nearest_kernel(place_ref, counts_ref, own_ref, sib_ref, keys_ref, out_ref):
    cluster, chip, core = place_ref[0], place_ref[1], place_ref[2]
    chips, rows, _ = keys_ref.shape
    groups = counts_ref.shape[0]
    slots = rows // groups
    column = lax.broadcasted_iota(jnp.int32, counts_ref.shape, 1)
    sizes = jnp.sum(jnp.where(column == cluster, counts_ref[...], 0), axis=1, keepdims=True)
    sizes = jnp.concatenate([sizes] * slots, axis=0)
    row = lax.broadcasted_iota(jnp.int32, (rows, 1), 0)
    lane = lax.broadcasted_iota(jnp.int32, (1, rows), 1)
    own_pos = (chip * CORES + core) * rows + lane
    sib_pos = (chip * CORES + 1 - core) * rows + lane
    own_best = jnp.full((1, rows), -1.0, jnp.float32)
    sib_best = jnp.full((1, rows), -1.0, jnp.float32)
    for block in range(chips):
        start = (block * CORES + core) * rows
        slot = (start + row) // groups
        key_pos = jnp.where(slot < sizes, start + row, FAR)
        keys = keys_ref[block]
        for_own = lax.dot_general(
            keys, own_ref[...], (((1,), (1,)), ((), ())), preferred_element_type=jnp.float32
        )
        for_own = jnp.where(key_pos < own_pos, for_own, -1.0)
        own_best = jnp.maximum(own_best, jnp.max(for_own, axis=0, keepdims=True))
        for_sib = lax.dot_general(
            keys, sib_ref[...], (((1,), (1,)), ((), ())), preferred_element_type=jnp.float32
        )
        for_sib = jnp.where(key_pos < sib_pos, for_sib, -1.0)
        sib_best = jnp.maximum(sib_best, jnp.max(for_sib, axis=0, keepdims=True))
    out_ref[0:1, :] = own_best
    out_ref[1:2, :] = sib_best


def nearest_partial(place, counts, own, sib, keys):
    rows, width = own.shape
    chips = keys.shape[0]
    flops = 2 * 2 * chips * rows * rows * width
    moved = 2 * width * rows * (chips + 2)
    vmem = pl.BlockSpec(memory_space=pltpu.VMEM)
    return pl.pallas_call(
        nearest_kernel,
        out_shape=jax.ShapeDtypeStruct((2, rows), jnp.float32),
        in_specs=[pl.BlockSpec(memory_space=pltpu.SMEM), vmem, vmem, vmem, vmem],
        out_specs=vmem,
        compiler_params=pltpu.CompilerParams(vmem_limit_bytes=32 << 20),
        cost_estimate=pl.CostEstimate(flops=flops, bytes_accessed=moved, transcendentals=0),
    )(place, counts, own, sib, keys)


def make_on_device(members):
    chips = members // CORES
    swap = [(m, m ^ 1) for m in range(members)]
    rings = [[chip * CORES + core for chip in range(chips)] for core in range(CORES)]

    def on_device(embeddings, counts):
        cluster = lax.axis_index("grp")
        member = lax.axis_index("mem")
        slot_dev = embeddings.shape[1]
        groups = embeddings.shape[2]
        width = embeddings.shape[3]
        local = embeddings.reshape(slot_dev, groups, width)
        values = local.astype(jnp.float32)
        units = (
            values * lax.rsqrt(jnp.sum(values * values, axis=-1, keepdims=True) + EPS)
        ).astype(jnp.bfloat16)
        owned = lax.all_to_all(units, "grp", split_axis=1, concat_axis=1, tiled=True)
        nrows = slot_dev * groups
        rows = owned.reshape(nrows, width)
        sib = lax.ppermute(rows, "mem", swap)
        copies = jnp.broadcast_to(rows[None], (chips, nrows, width))
        keys = lax.all_to_all(
            copies, "mem", split_axis=0, concat_axis=0, tiled=True, axis_index_groups=rings
        )
        place = jnp.stack([cluster, member // CORES, member % CORES]).astype(jnp.int32)
        best = nearest_partial(place, counts, rows, sib, keys)
        best = jnp.maximum(best[0], lax.ppermute(best[1], "mem", swap))
        back = lax.all_to_all(
            best.reshape(slot_dev, groups), "grp", split_axis=1, concat_axis=1, tiled=True
        )
        return back.reshape(1, slot_dev, groups)

    return on_device


def solution(mesh):
    return jax.shard_map(
        make_on_device(mesh.shape["mem"]),
        mesh=mesh,
        in_specs=(P("grp", "mem", None, None), P()),
        out_specs=P("grp", "mem", None),
        check_vma=False,
    )
```

time: 124 us -> 100 us (0.81)
  the two profiles are of different devices: /device:TPU:24 before, /device:TPU:1 now
where the time goes in v1:
time: 100 us; the launch traced here: 99.7 us
  blocking collectives  64.5 us (64%)
  starting transfers between devices  16.3 us (16%)
  waiting for transfers between devices  12.3 us (12%)
  other arithmetic  2.78 us (3%)
  local copies, waits for them, and re-layouts  2.15 us (2%)
  Pallas kernels  1.57 us (2%)
    all_to_all x1, blocking collectives, on_device(): lax.all_to_all(units, 'grp', split_axis=1, concat_axis=1, tiled=True)  43.8 us
    all_to_all x1, blocking collectives, on_device(): lax.all_to_all(best.reshape(slot_dev, groups), 'grp', split_axis=1, conca...  20.7 us
    all_to_all x1, waiting for transfers between devices, on_device(): lax.all_to_all(copies, 'mem', split_axis=0, concat_axis=0, tiled=True, ax...  10.2 us
    ppermute x1, starting transfers between devices, on_device(): best = jnp.maximum(best[0], lax.ppermute(best[1], 'mem', swap))  6.47 us
    ppermute x1, starting transfers between devices, on_device(): sib = lax.ppermute(rows, 'mem', swap)  5.54 us
    all_to_all x1, starting transfers between devices, on_device(): lax.all_to_all(copies, 'mem', split_axis=0, concat_axis=0, tiled=True, ax...  4.31 us
  transfers between devices with their start and end apart: 3, of which 3 were waited for; matrix products, arithmetic and copies ran while one was open for 0% of the time, Pallas kernels for 0%

profile of v1, /device:TPU:1, one launch (start us, length us, event | category | flops | bytes accessed | tf_op | source)
XLA Modules:
  0.0 99.7 jit_solution(2632892683370059166)
XLA Ops:
  0.0 1.4 %fusion = f32[4,64]{0,1:T(8,128)S(1)} fusion(bf16[1,4,64,768]{3,2,1,0:T(8,128)(2,1)} %param.2), kind=kLoop, calls=%fused_computation.2 | loop fusion | flops 589568 | bytes 394240 | tf_op jit(solution)/shard_map/reduce_sum | solution.py:76
  1.4 1.3 %fusion.1 = bf16[4,64,768]{2,0,1:T(4,128)(2,1)S(1)} fusion(f32[4,64]{0,1:T(8,128)S(1)} %add_rsqrt_fusion, bf16[1,4,64,768]{3,2,1,0:T(8,128)(2,1)} %param.2), kind=kLoop, calls=%fused_computation.3 | loop fusion | flops 589824 | bytes 787456 | tf_op jit(solution)/shard_map/convert_element_type | solution.py:77
  2.7 43.8 %all_to_all.19 = bf16[4,64,768]{2,0,1:T(4,128)(2,1)S(1)} all-to-all(bf16[4,64,768]{2,0,1:T(4,128)(2,1)S(1)} %fusion.1), channel_id=1, replica_groups=mesh['grp'=64,'mem'=8] {'grp'}, dimensions={1} | all-to-all | bytes 786432 | tf_op jit(solution)/shard_map/all_to_all | solution.py:78
  46.6 1.3 %broadcast_in_dim.2 = bf16[4,256,768]{2,1,0:T(8,128)(2,1)} broadcast(bf16[256,768]{1,0:T(8,128)(2,1)S(1)} %bitcast.11), dimensions={1,2} | broadcast | bytes 1966080 | tf_op jit(solution)/shard_map/broadcast_in_dim | solution.py:82
  47.9 0.0 copy-start
  47.9 4.3 %all-to-all-start.1 = ((bf16[4,256,768]{2,1,0:T(8,128)(2,1)}), bf16[4,256,768]{2,1,0:T(8,128)(2,1)S(1)}, u32[]{:S(2)}, u32[]{:S(2)}) async-start(bf16[4,256,768]{2,1,0:T(8,128)(2,1)} %broadcast_in_dim.2), calls=%async_computation.1 | async-start | bytes 3145728 | tf_op jit(solution)/shard_map/all_to_all | solution.py:83
  52.2 5.5 %collective-permute-start = (bf16[256,768]{1,0:T(8,128)(2,1)S(1)}, bf16[256,768]{1,0:T(8,128)(2,1)S(1)}, u32[]{:S(2)}, u32[]{:S(2)}) collective-permute-start(bf16[256,768]{1,0:T(8,128)(2,1)S(1)} %bitcast.12), channel_id=1, source_target_pairs={{0,1},{1,0},{2,3},{3,2},{4,5},{5,4},{6,7},{7,6},{8,9},{9,8},{10,11... | collective-permute-start | bytes 1179656 | tf_op jit(solution)/shard_map/ppermute | solution.py:81
  57.7 0.1 pad_add_fusion.place_ref
  57.8 1.2 %collective-permute-done.sib_ref = bf16[256,768]{1,0:T(8,128)(2,1)S(1)} collective-permute-done((bf16[256,768]{1,0:T(8,128)(2,1)S(1)}, bf16[256,768]{1,0:T(8,128)(2,1)S(1)}, u32[]{:S(2)}, u32[]{:S(2)}) %collective-permute-start) | collective-permute-done | bytes 393248 | tf_op jit(solution)/shard_map/ppermute | solution.py:81
  59.0 10.2 %all-to-all-done.1.keys_ref = bf16[4,256,768]{2,1,0:T(8,128)(2,1)S(1)} async-done(((bf16[4,256,768]{2,1,0:T(8,128)(2,1)}), bf16[4,256,768]{2,1,0:T(8,128)(2,1)S(1)}, u32[]{:S(2)}, u32[]{:S(2)}) %all-to-all-start.1) | async-done | bytes 1572896 | tf_op jit(solution)/shard_map/all_to_all | solution.py:83
  69.3 0.0 copy-done
  69.3 1.6 %shard_map.28 = f32[2,256]{1,0:T(2,128)S(1)} custom-call(s32[3]{0:T(128)S(1)} %pad_add_fusion.place_ref, s32[64,64]{1,0:T(8,128)S(1)} %copy-done, bf16[256,768]{1,0:T(8,128)(2,1)S(1)} %bitcast.13, bf16[256,768]{1,0:T(8,128)(2,1)S(1)} %collective-permute-done.sib_ref, bf16[4,256,768]{2,1,0:T(8,128)(2,1)S(1)} %all-to-all-done.1.keys_ref), custom_call_target="tpu_custom_call" | custom-call | flops 805306368 | bytes 2359296 | tf_op jit(solution)/shard_map/pallas_call | solution.py:52
  70.9 6.5 %collective-permute-start.1 = (f32[256]{0:T(256)S(1)}, f32[256]{0:T(256)S(1)}, u32[]{:S(2)}, u32[]{:S(2)}) collective-permute-start(f32[256]{0:T(256)S(1)} %bitcast.16), channel_id=1, source_target_pairs={{0,1},{1,0},{2,3},{3,2},{4,5},{5,4},{6,7},{7,6},{8,9},{9,8},{10,11... | collective-permute-start | bytes 3080 | tf_op jit(solution)/shard_map/ppermute | solution.py:88
  77.4 0.8 collective-permute-done.1
  78.2 0.1 all_to_all.14
  78.2 0.1 copy.8
  78.3 20.7 %all_to_all.20 = f32[4,64,1]{0,2,1:T(1,128)S(1)} all-to-all(f32[4,64,1]{0,2,1:T(1,128)S(1)} %copy.8), channel_id=1, replica_groups=mesh['grp'=64,'mem'=8] {'grp'}, dimensions={1} | all-to-all | bytes 2048 | tf_op jit(solution)/shard_map/all_to_all | solution.py:89
  99.0 0.7 copy.9
  (4 shorter events, 0.1 us)
Async XLA Ops:
  47.9 21.4 %copy-start = (s32[64,64]{1,0:T(8,128)S(1)}, s32[64,64]{1,0:T(8,128)}, u32[]{:S(2)}) copy-start(s32[64,64]{1,0:T(8,128)} %counts_ref.1) | copy-start | bytes 49156
  47.9 21.4 %all-to-all-start.1 = ((bf16[4,256,768]{2,1,0:T(8,128)(2,1)}), bf16[4,256,768]{2,1,0:T(8,128)(2,1)S(1)}, u32[]{:S(2)}, u32[]{:S(2)}) async-start(bf16[4,256,768]{2,1,0:T(8,128)(2,1)} %broadcast_in_dim.2), calls=%async_computation.1 | async-start | bytes 3145728 | tf_op jit(solution)/shard_map/all_to_all | solution.py:83
  52.2 6.9 %collective-permute-start = (bf16[256,768]{1,0:T(8,128)(2,1)S(1)}, bf16[256,768]{1,0:T(8,128)(2,1)S(1)}, u32[]{:S(2)}, u32[]{:S(2)}) collective-permute-start(bf16[256,768]{1,0:T(8,128)(2,1)S(1)} %bitcast.12), channel_id=1, source_target_pairs={{0,1},{1,0},{2,3},{3,2},{4,5},{5,4},{6,7},{7,6},{8,9},{9,8},{10,11... | collective-permute-start | bytes 1179656 | tf_op jit(solution)/shard_map/ppermute | solution.py:81
  70.9 7.3 %collective-permute-start.1 = (f32[256]{0:T(256)S(1)}, f32[256]{0:T(256)S(1)}, u32[]{:S(2)}, u32[]{:S(2)}) collective-permute-start(f32[256]{0:T(256)S(1)} %bitcast.16), channel_id=1, source_target_pairs={{0,1},{1,0},{2,3},{3,2},{4,5},{5,4},{6,7},{7,6},{8,9},{9,8},{10,11... | collective-permute-start | bytes 3080 | tf_op jit(solution)/shard_map/ppermute | solution.py:88

commit v2 on v1

v2 whole, which is shorter than its diff:
```python
import jax
import jax.numpy as jnp
from jax import lax
from jax.experimental import pallas as pl
from jax.experimental.pallas import tpu as pltpu
from jax.sharding import PartitionSpec as P

EPS = 1e-06
FAR = 1 << 20
CORE, NEXT, CROSS = 1, 2, 6


def nearest_kernel(place_ref, counts_ref, query_ref, *refs):
    keys_refs, out_ref = refs[:-1], refs[-1]
    cluster, query_member = place_ref[0], place_ref[1]
    rows = query_ref.shape[0]
    groups = counts_ref.shape[0]
    slots = rows // groups
    column = lax.broadcasted_iota(jnp.int32, counts_ref.shape, 1)
    sizes = jnp.sum(jnp.where(column == cluster, counts_ref[...], 0), axis=1, keepdims=True)
    sizes = jnp.concatenate([sizes] * slots, axis=0)
    row = lax.broadcasted_iota(jnp.int32, (rows, 1), 0)
    lane = lax.broadcasted_iota(jnp.int32, (1, rows), 1)
    query_pos = query_member * rows + lane
    best = jnp.full((1, rows), -1.0, jnp.float32)
    for index, keys_ref in enumerate(keys_refs):
        start = place_ref[2 + index] * rows
        slot = (start + row) // groups
        key_pos = jnp.where(slot < sizes, start + row, FAR)
        score = lax.dot_general(
            keys_ref[...], query_ref[...], (((1,), (1,)), ((), ())), preferred_element_type=jnp.float32
        )
        score = jnp.where(key_pos < query_pos, score, -1.0)
        best = jnp.maximum(best, jnp.max(score, axis=0, keepdims=True))
    out_ref[...] = best


def nearest_of(cluster, counts, query, query_member, keys, key_members):
    rows, width = query.shape
    place = jnp.stack([cluster, query_member, *key_members]).astype(jnp.int32)
    flops = 2 * len(keys) * rows * rows * width
    moved = 2 * width * rows * (len(keys) + 1)
    vmem = pl.BlockSpec(memory_space=pltpu.VMEM)
    return pl.pallas_call(
        nearest_kernel,
        out_shape=jax.ShapeDtypeStruct((1, rows), jnp.float32),
        in_specs=[pl.BlockSpec(memory_space=pltpu.SMEM)] + [vmem] * (2 + len(keys)),
        out_specs=vmem,
        compiler_params=pltpu.CompilerParams(vmem_limit_bytes=32 << 20),
        cost_estimate=pl.CostEstimate(flops=flops, bytes_accessed=moved, transcendentals=0),
    )(place, counts, query, *keys)


def make_on_device(members):
    def trade(array, mask):
        return lax.ppermute(array, "mem", [(m, m ^ mask) for m in range(members)])

    def on_device(embeddings, counts):
        cluster = lax.axis_index("grp")
        member = lax.axis_index("mem")
        slot_dev = embeddings.shape[1]
        groups = embeddings.shape[2]
        width = embeddings.shape[3]
        local = embeddings.reshape(slot_dev, groups, width)
        values = local.astype(jnp.float32)
        units = (
            values * lax.rsqrt(jnp.sum(values * values, axis=-1, keepdims=True) + EPS)
        ).astype(jnp.bfloat16)
        owned = lax.all_to_all(units, "grp", split_axis=1, concat_axis=1, tiled=True)
        rows = owned.reshape(slot_dev * groups, width)
        next_rows = trade(rows, NEXT)
        cross_rows = trade(rows, CROSS)
        sib_rows = trade(rows, CORE)
        next_sib_rows = trade(next_rows, CORE)
        keys = (rows, sib_rows, next_rows, next_sib_rows)
        key_members = (member, member ^ CORE, member ^ NEXT, member ^ NEXT ^ CORE)
        cross_best = nearest_of(cluster, counts, cross_rows, member ^ CROSS, keys, key_members)
        from_cross = trade(cross_best, CROSS)
        own_best = nearest_of(cluster, counts, rows, member, keys, key_members)
        best = jnp.maximum(own_best, from_cross)
        back = lax.all_to_all(
            best.reshape(slot_dev, groups), "grp", split_axis=1, concat_axis=1, tiled=True
        )
        return back.reshape(1, slot_dev, groups)

    return on_device


def solution(mesh):
    return jax.shard_map(
        make_on_device(mesh.shape["mem"]),
        mesh=mesh,
        in_specs=(P("grp", "mem", None, None), P()),
        out_specs=P("grp", "mem", None),
        check_vma=False,
    )
```

time: 100 us -> 92.6 us (0.926)
  the two profiles are of different devices: /device:TPU:1 before, /device:TPU:24 now
where the time goes in v2:
time: 92.6 us; the launch traced here: 92.2 us
  blocking collectives  67.9 us (73%)
  starting transfers between devices  12.4 us (13%)
  waiting for transfers between devices  6.39 us (7%)
  Pallas kernels  2.58 us (3%)
  other arithmetic  1.8 us (2%)
  local copies, waits for them, and re-layouts  1.06 us (1%)
    all_to_all x1, blocking collectives, on_device(): lax.all_to_all(units, 'grp', split_axis=1, concat_axis=1, tiled=True)  45.7 us
    all_to_all x1, blocking collectives, on_device(): lax.all_to_all(best.reshape(slot_dev, groups), 'grp', split_axis=1, conca...  22.2 us
    ppermute x5, starting transfers between devices, trade(): return lax.ppermute(array, 'mem', [(m, m ^ mask) for m in range(members)])  12.4 us
    ppermute x5, waiting for transfers between devices, trade(): return lax.ppermute(array, 'mem', [(m, m ^ mask) for m in range(members)])  6.39 us
    pallas_call x2, Pallas kernels, nearest_of(): pl.pallas_call(nearest_kernel, out_shape=jax.ShapeDtypeStruct((1, rows),...  2.58 us
  transfers between devices with their start and end apart: 5, of which 3 were waited for; matrix products, arithmetic and copies ran while one was open for 0% of the time, Pallas kernels for 1%

profile of v2, /device:TPU:24, one launch (start us, length us, event | category | flops | bytes accessed | tf_op | source)
XLA Modules:
  0.0 92.2 jit_solution(555144948584218340)
XLA Ops:
  0.0 0.0 copy-start.1
  0.0 1.4 %fusion = f32[4,64]{0,1:T(8,128)S(1)} fusion(bf16[1,4,64,768]{3,2,1,0:T(8,128)(2,1)} %param.2), kind=kLoop, calls=%fused_computation.2 | loop fusion | flops 589568 | bytes 394240 | tf_op jit(solution)/shard_map/reduce_sum | solution.py:67
  1.4 0.0 copy-done.1
  1.5 0.3 fusion.1
  1.8 45.7 %all_to_all.14 = bf16[4,64,768]{2,0,1:T(4,128)(2,1)S(1)} all-to-all(bf16[4,64,768]{2,0,1:T(4,128)(2,1)S(1)} %fusion.1), channel_id=1, replica_groups=mesh['grp'=64,'mem'=8] {'grp'}, dimensions={1} | all-to-all | bytes 786432 | tf_op jit(solution)/shard_map/all_to_all | solution.py:69
  47.5 0.0 copy-start
  47.5 2.7 %collective-permute-start.1 = (bf16[256,768]{1,0:T(8,128)(2,1)S(1)}, bf16[256,768]{1,0:T(8,128)(2,1)S(1)}, u32[]{:S(2)}, u32[]{:S(2)}) collective-permute-start(bf16[256,768]{1,0:T(8,128)(2,1)S(1)} %bitcast.12), channel_id=1, source_target_pairs={{0,2},{1,3},{2,0},{3,1},{4,6},{5,7},{6,4},{7,5},{8,10},{9,11},{10,... | collective-permute-start | bytes 1179656 | tf_op jit(solution)/shard_map/ppermute | solution.py:56
  50.2 3.0 %collective-permute-start.3 = (bf16[256,768]{1,0:T(8,128)(2,1)S(1)}, bf16[256,768]{1,0:T(8,128)(2,1)S(1)}, u32[]{:S(2)}, u32[]{:S(2)}) collective-permute-start(bf16[256,768]{1,0:T(8,128)(2,1)S(1)} %bitcast.13), channel_id=1, source_target_pairs={{0,6},{1,7},{2,4},{3,5},{4,2},{5,3},{6,0},{7,1},{8,14},{9,15},{10,... | collective-permute-start | bytes 1179656 | tf_op jit(solution)/shard_map/ppermute | solution.py:56
  53.2 1.9 %collective-permute-start = (bf16[256,768]{1,0:T(8,128)(2,1)S(1)}, bf16[256,768]{1,0:T(8,128)(2,1)S(1)}, u32[]{:S(2)}, u32[]{:S(2)}) collective-permute-start(bf16[256,768]{1,0:T(8,128)(2,1)S(1)} %bitcast.14), channel_id=1, source_target_pairs={{0,1},{1,0},{2,3},{3,2},{4,5},{5,4},{6,7},{7,6},{8,9},{9,8},{10,11... | collective-permute-start | bytes 1179656 | tf_op jit(solution)/shard_map/ppermute | solution.py:56
  55.1 2.5 %collective-permute-done.1.refs_2_ = bf16[256,768]{1,0:T(8,128)(2,1)S(1)} collective-permute-done((bf16[256,768]{1,0:T(8,128)(2,1)S(1)}, bf16[256,768]{1,0:T(8,128)(2,1)S(1)}, u32[]{:S(2)}, u32[]{:S(2)}) %collective-permute-start.1) | collective-permute-done | bytes 393248 | tf_op jit(solution)/shard_map/ppermute | solution.py:56
  57.6 1.9 %collective-permute-start.2 = (bf16[256,768]{1,0:T(8,128)(2,1)S(1)}, bf16[256,768]{1,0:T(8,128)(2,1)S(1)}, u32[]{:S(2)}, u32[]{:S(2)}) collective-permute-start(bf16[256,768]{1,0:T(8,128)(2,1)S(1)} %collective-permute-done.1.refs_2_), channel_id=1, source_target_pairs={{0,1},{1,0},{2,3},{3,2},{4,5},{5,4},{6,7},{7,6},{8,9},{9,8},{10,11... | collective-permute-start | bytes 1179656 | tf_op jit(solution)/shard_map/ppermute | solution.py:56
  59.5 0.1 stack.35.place_ref
  59.6 0.1 stack.37.place_ref
  59.7 1.5 %collective-permute-done.3.query_ref = bf16[256,768]{1,0:T(8,128)(2,1)S(1)} collective-permute-done((bf16[256,768]{1,0:T(8,128)(2,1)S(1)}, bf16[256,768]{1,0:T(8,128)(2,1)S(1)}, u32[]{:S(2)}, u32[]{:S(2)}) %collective-permute-start.3) | collective-permute-done | bytes 393248 | tf_op jit(solution)/shard_map/ppermute | solution.py:56
  61.2 0.0 collective-permute-done.refs_1_
  61.2 0.0 collective-permute-done.2.refs_3_
  61.2 0.0 copy-done
  61.2 1.3 %shard_map.29 = f32[1,256]{1,0:T(1,128)S(1)} custom-call(s32[6]{0:T(128)S(1)} %stack.37.place_ref, s32[64,64]{1,0:T(8,128)S(1)} %copy-done, bf16[256,768]{1,0:T(8,128)(2,1)S(1)} %collective-permute-done.3.query_ref, bf16[256,768]{1,0:T(8,128)(2,1)S(1)} %bitcast.15, bf16[256,768]{1,0:T(8,128)(2,1)S(1)} %collective-permute-done.refs_1_, ...), custom_call_target="tpu_custom_call" | custom-call | flops 402653184 | bytes 1966080 | tf_op jit(solution)/shard_map/pallas_call | solution.py:44
  62.5 3.0 %collective-permute-start.4 = (f32[1,256]{1,0:T(1,128)S(1)}, f32[1,256]{1,0:T(1,128)S(1)}, u32[]{:S(2)}, u32[]{:S(2)}) collective-permute-start(f32[1,256]{1,0:T(1,128)S(1)} %shard_map.29), channel_id=1, source_target_pairs={{0,6},{1,7},{2,4},{3,5},{4,2},{5,3},{6,0},{7,1},{8,14},{9,15},{10,... | collective-permute-start | bytes 3080 | tf_op jit(solution)/shard_map/ppermute | solution.py:56
  65.5 1.3 %shard_map.28 = f32[1,256]{1,0:T(1,128)S(1)} custom-call(s32[6]{0:T(128)S(1)} %stack.35.place_ref, s32[64,64]{1,0:T(8,128)S(1)} %copy-done, bf16[256,768]{1,0:T(8,128)(2,1)S(1)} %bitcast.16, bf16[256,768]{1,0:T(8,128)(2,1)S(1)} %bitcast.17, bf16[256,768]{1,0:T(8,128)(2,1)S(1)} %collective-permute-done.refs_1_, ...), custom_call_target="tpu_custom_call" | custom-call | flops 402653184 | bytes 1966080 | tf_op jit(solution)/shard_map/pallas_call | solution.py:44
  66.8 2.4 %collective-permute-done.4 = f32[1,256]{1,0:T(1,128)S(1)} collective-permute-done((f32[1,256]{1,0:T(1,128)S(1)}, f32[1,256]{1,0:T(1,128)S(1)}, u32[]{:S(2)}, u32[]{:S(2)}) %collective-permute-start.4) | collective-permute-done | bytes 1056 | tf_op jit(solution)/shard_map/ppermute | solution.py:56
  69.2 0.1 all_to_all.10
  69.3 0.1 copy.5
  69.4 22.2 %all_to_all.15 = f32[4,64,1]{0,2,1:T(1,128)S(1)} all-to-all(f32[4,64,1]{0,2,1:T(1,128)S(1)} %copy.5), channel_id=1, replica_groups=mesh['grp'=64,'mem'=8] {'grp'}, dimensions={1} | all-to-all | bytes 2048 | tf_op jit(solution)/shard_map/all_to_all | solution.py:81
  91.6 0.7 copy.6
  (3 shorter events, 0.1 us)
Async XLA Ops:
  0.0 1.4 %copy-start.1 = (bf16[1,4,64,768]{3,2,1,0:T(8,128)(2,1)S(1)}, bf16[1,4,64,768]{3,2,1,0:T(8,128)(2,1)}, u32[]{:S(2)}) copy-start(bf16[1,4,64,768]{3,2,1,0:T(8,128)(2,1)} %param.2) | copy-start | bytes 1179652
  47.5 13.7 %copy-start = (s32[64,64]{1,0:T(8,128)S(1)}, s32[64,64]{1,0:T(8,128)}, u32[]{:S(2)}) copy-start(s32[64,64]{1,0:T(8,128)} %counts_ref.3) | copy-start | bytes 49156
  47.5 10.1 %collective-permute-start.1 = (bf16[256,768]{1,0:T(8,128)(2,1)S(1)}, bf16[256,768]{1,0:T(8,128)(2,1)S(1)}, u32[]{:S(2)}, u32[]{:S(2)}) collective-permute-start(bf16[256,768]{1,0:T(8,128)(2,1)S(1)} %bitcast.12), channel_id=1, source_target_pairs={{0,2},{1,3},{2,0},{3,1},{4,6},{5,7},{6,4},{7,5},{8,10},{9,11},{10,... | collective-permute-start | bytes 1179656 | tf_op jit(solution)/shard_map/ppermute | solution.py:56
  50.2 11.0 %collective-permute-start.3 = (bf16[256,768]{1,0:T(8,128)(2,1)S(1)}, bf16[256,768]{1,0:T(8,128)(2,1)S(1)}, u32[]{:S(2)}, u32[]{:S(2)}) collective-permute-start(bf16[256,768]{1,0:T(8,128)(2,1)S(1)} %bitcast.13), channel_id=1, source_target_pairs={{0,6},{1,7},{2,4},{3,5},{4,2},{5,3},{6,0},{7,1},{8,14},{9,15},{10,... | collective-permute-start | bytes 1179656 | tf_op jit(solution)/shard_map/ppermute | solution.py:56
  53.2 8.0 %collective-permute-start = (bf16[256,768]{1,0:T(8,128)(2,1)S(1)}, bf16[256,768]{1,0:T(8,128)(2,1)S(1)}, u32[]{:S(2)}, u32[]{:S(2)}) collective-permute-start(bf16[256,768]{1,0:T(8,128)(2,1)S(1)} %bitcast.14), channel_id=1, source_target_pairs={{0,1},{1,0},{2,3},{3,2},{4,5},{5,4},{6,7},{7,6},{8,9},{9,8},{10,11... | collective-permute-start | bytes 1179656 | tf_op jit(solution)/shard_map/ppermute | solution.py:56
  57.6 3.6 %collective-permute-start.2 = (bf16[256,768]{1,0:T(8,128)(2,1)S(1)}, bf16[256,768]{1,0:T(8,128)(2,1)S(1)}, u32[]{:S(2)}, u32[]{:S(2)}) collective-permute-start(bf16[256,768]{1,0:T(8,128)(2,1)S(1)} %collective-permute-done.1.refs_2_), channel_id=1, source_target_pairs={{0,1},{1,0},{2,3},{3,2},{4,5},{5,4},{6,7},{7,6},{8,9},{9,8},{10,11... | collective-permute-start | bytes 1179656 | tf_op jit(solution)/shard_map/ppermute | solution.py:56
  62.5 6.7 %collective-permute-start.4 = (f32[1,256]{1,0:T(1,128)S(1)}, f32[1,256]{1,0:T(1,128)S(1)}, u32[]{:S(2)}, u32[]{:S(2)}) collective-permute-start(f32[1,256]{1,0:T(1,128)S(1)} %shard_map.29), channel_id=1, source_target_pairs={{0,6},{1,7},{2,4},{3,5},{4,2},{5,3},{6,0},{7,1},{8,14},{9,15},{10,... | collective-permute-start | bytes 3080 | tf_op jit(solution)/shard_map/ppermute | solution.py:56

commit v3 on v2

v3 whole, which is shorter than its diff:
```python
import jax
import jax.numpy as jnp
from jax import lax
from jax.experimental import pallas as pl
from jax.experimental.pallas import tpu as pltpu
from jax.sharding import PartitionSpec as P

EPS = 1e-06
FAR = 1 << 20
LANES = 128
CORE, NEXT, CROSS = 1, 2, 6


def nearest_kernel(place_ref, counts_ref, own_ref, sib_ref, cross_ref, next_ref, next_sib_ref, out_ref):
    cluster, member = place_ref[0], place_ref[1]
    rows = own_ref.shape[0]
    groups = counts_ref.shape[0]
    slots = rows // groups
    column = lax.broadcasted_iota(jnp.int32, counts_ref.shape, 1)
    sizes = jnp.sum(jnp.where(column == cluster, counts_ref[...], 0), axis=1, keepdims=True)
    sizes = jnp.broadcast_to(sizes.astype(jnp.float32), (groups, LANES))
    sizes = jnp.transpose(sizes)[0:1, :].astype(jnp.int32)
    sizes = jnp.concatenate([sizes] * slots, axis=1)
    lane = lax.broadcasted_iota(jnp.int32, (1, rows), 1)
    row = lax.broadcasted_iota(jnp.int32, (rows, 1), 0)

    keys = []
    for key_ref, mask in ((own_ref, 0), (sib_ref, CORE), (next_ref, NEXT), (next_sib_ref, NEXT ^ CORE)):
        start = (member ^ mask) * rows
        slot = (start + lane) // groups
        keys.append((key_ref, jnp.where(slot < sizes, start + lane, FAR)))
    results = []
    for query_ref, mask in ((own_ref, 0), (cross_ref, CROSS)):
        query_pos = (member ^ mask) * rows + row
        best = jnp.full((rows, LANES), -1.0, jnp.float32)
        for key_ref, key_pos in keys:
            score = lax.dot_general(
                query_ref[...], key_ref[...], (((1,), (1,)), ((), ())), preferred_element_type=jnp.float32
            )
            score = jnp.where(key_pos < query_pos, score, -1.0)
            for first in range(0, rows, LANES):
                best = jnp.maximum(best, score[:, first : first + LANES])
        best = jnp.max(best, axis=1, keepdims=True)
        results.append(
            jnp.concatenate([best[t * groups : (t + 1) * groups] for t in range(slots)], axis=1)
        )
    own_low = member < (member ^ CROSS)
    out_ref[:groups, 0, :] = jnp.where(own_low, results[0], results[1])
    out_ref[groups:, 0, :] = jnp.where(own_low, results[1], results[0])


def nearest_of(place, counts, own, cross, sib, nxt, next_sib):
    rows, width = own.shape
    groups = counts.shape[0]
    vmem = pl.BlockSpec(memory_space=pltpu.VMEM)
    return pl.pallas_call(
        nearest_kernel,
        out_shape=jax.ShapeDtypeStruct((2 * groups, 1, rows // groups), jnp.float32),
        in_specs=[pl.BlockSpec(memory_space=pltpu.SMEM)] + [vmem] * 6,
        out_specs=vmem,
        compiler_params=pltpu.CompilerParams(vmem_limit_bytes=32 << 20),
        cost_estimate=pl.CostEstimate(
            flops=16 * rows * rows * width, bytes_accessed=10 * rows * width, transcendentals=0
        ),
    )(place, counts, own, sib, cross, nxt, next_sib)


def make_on_device(clusters, members):
    def trade(array, mask):
        return lax.ppermute(array, "mem", [(m, m ^ mask) for m in range(members)])

    lows = [m for m in range(members) if m < m ^ CROSS]
    returns = [
        [c * members + m for m in (low, low ^ CROSS) for c in range(clusters)] for low in lows
    ]

    def on_device(embeddings, counts):
        cluster = lax.axis_index("grp")
        member = lax.axis_index("mem")
        slot_dev = embeddings.shape[1]
        groups = embeddings.shape[2]
        width = embeddings.shape[3]
        local = embeddings.reshape(slot_dev, groups, width)
        values = local.astype(jnp.float32)
        units = (
            values * lax.rsqrt(jnp.sum(values * values, axis=-1, keepdims=True) + EPS)
        ).astype(jnp.bfloat16)
        owned = lax.all_to_all(units, "grp", split_axis=1, concat_axis=1, tiled=True)
        rows = owned.reshape(slot_dev * groups, width)
        next_rows = trade(rows, NEXT)
        cross_rows = trade(rows, CROSS)
        sib_rows = trade(rows, CORE)
        next_sib_rows = trade(next_rows, CORE)
        place = jnp.stack([cluster, member]).astype(jnp.int32)
        best = nearest_of(place, counts, rows, cross_rows, sib_rows, next_rows, next_sib_rows)
        back = lax.all_to_all(
            best, ("grp", "mem"), split_axis=0, concat_axis=0, tiled=True, axis_index_groups=returns
        )
        back = jnp.max(back.reshape(2, groups, slot_dev), axis=0)
        return back.T.reshape(1, slot_dev, groups)

    return on_device


def solution(mesh):
    return jax.shard_map(
        make_on_device(mesh.shape["grp"], mesh.shape["mem"]),
        mesh=mesh,
        in_specs=(P("grp", "mem", None, None), P()),
        out_specs=P("grp", "mem", None),
        check_vma=False,
    )
```

time: 92.6 us -> 91.6 us (0.989)
  the two profiles are of different devices: /device:TPU:24 before, /device:TPU:1 now
where the time goes in v3:
time: 91.6 us; the launch traced here: 91.3 us
  blocking collectives  70.5 us (77%)
  starting transfers between devices  15.3 us (17%)
  other arithmetic  1.86 us (2%)
  Pallas kernels  1.66 us (2%)
  waiting for transfers between devices  1.25 us (1%)
    all_to_all x1, blocking collectives, on_device(): lax.all_to_all(units, 'grp', split_axis=1, concat_axis=1, tiled=True)  43.8 us
    all_to_all x1, blocking collectives, on_device(): lax.all_to_all(best, ('grp', 'mem'), split_axis=0, concat_axis=0, tiled=T...  26.6 us
    ppermute x4, starting transfers between devices, trade(): return lax.ppermute(array, 'mem', [(m, m ^ mask) for m in range(members)])  15.3 us
  transfers between devices with their start and end apart: 4, of which 1 were waited for; matrix products, arithmetic and copies ran while one was open for 0% of the time, Pallas kernels for 0%

profile of v3, /device:TPU:1, one launch (start us, length us, event | category | flops | bytes accessed | tf_op | source)
XLA Modules:
  0.0 91.3 jit_solution(17375991015141113218)
XLA Ops:
  0.0 0.0 copy-start.1
  0.0 1.4 %fusion = f32[4,64]{0,1:T(8,128)S(1)} fusion(bf16[1,4,64,768]{3,2,1,0:T(8,128)(2,1)} %param.2), kind=kLoop, calls=%fused_computation.2 | loop fusion | flops 589568 | bytes 394240 | tf_op jit(solution)/shard_map/reduce_sum | solution.py:86
  1.4 0.0 copy-done.1
  1.5 0.3 fusion.1
  1.8 43.8 %all_to_all.10 = bf16[4,64,768]{2,0,1:T(4,128)(2,1)S(1)} all-to-all(bf16[4,64,768]{2,0,1:T(4,128)(2,1)S(1)} %fusion.1), channel_id=1, replica_groups=mesh['grp'=64,'mem'=8] {'grp'}, dimensions={1} | all-to-all | bytes 786432 | tf_op jit(solution)/shard_map/all_to_all | solution.py:88
  45.6 0.0 copy-start
  45.7 3.2 %collective-permute-start.2 = (bf16[256,768]{1,0:T(8,128)(2,1)S(1)}, bf16[256,768]{1,0:T(8,128)(2,1)S(1)}, u32[]{:S(2)}, u32[]{:S(2)}) collective-permute-start(bf16[256,768]{1,0:T(8,128)(2,1)S(1)} %bitcast.13), channel_id=1, source_target_pairs={{0,2},{1,3},{2,0},{3,1},{4,6},{5,7},{6,4},{7,5},{8,10},{9,11},{10,... | collective-permute-start | bytes 1179656 | tf_op jit(solution)/shard_map/ppermute | solution.py:70
  48.9 3.8 %collective-permute-start.1 = (bf16[256,768]{1,0:T(8,128)(2,1)S(1)}, bf16[256,768]{1,0:T(8,128)(2,1)S(1)}, u32[]{:S(2)}, u32[]{:S(2)}) collective-permute-start(bf16[256,768]{1,0:T(8,128)(2,1)S(1)} %bitcast.14), channel_id=1, source_target_pairs={{0,6},{1,7},{2,4},{3,5},{4,2},{5,3},{6,0},{7,1},{8,14},{9,15},{10,... | collective-permute-start | bytes 1179656 | tf_op jit(solution)/shard_map/ppermute | solution.py:70
  52.7 5.8 %collective-permute-start = (bf16[256,768]{1,0:T(8,128)(2,1)S(1)}, bf16[256,768]{1,0:T(8,128)(2,1)S(1)}, u32[]{:S(2)}, u32[]{:S(2)}) collective-permute-start(bf16[256,768]{1,0:T(8,128)(2,1)S(1)} %bitcast.15), channel_id=1, source_target_pairs={{0,1},{1,0},{2,3},{3,2},{4,5},{5,4},{6,7},{7,6},{8,9},{9,8},{10,11... | collective-permute-start | bytes 1179656 | tf_op jit(solution)/shard_map/ppermute | solution.py:70
  58.5 0.0 collective-permute-done.2.next_ref
  58.5 2.4 %collective-permute-start.3 = (bf16[256,768]{1,0:T(8,128)(2,1)S(1)}, bf16[256,768]{1,0:T(8,128)(2,1)S(1)}, u32[]{:S(2)}, u32[]{:S(2)}) collective-permute-start(bf16[256,768]{1,0:T(8,128)(2,1)S(1)} %collective-permute-done.2.next_ref), channel_id=1, source_target_pairs={{0,1},{1,0},{2,3},{3,2},{4,5},{5,4},{6,7},{7,6},{8,9},{9,8},{10,11... | collective-permute-start | bytes 1179656 | tf_op jit(solution)/shard_map/ppermute | solution.py:70
  61.0 0.1 pad_add_fusion.place_ref
  61.1 0.0 collective-permute-done.1.cross_ref
  61.1 0.0 collective-permute-done.sib_ref
  61.1 1.2 %collective-permute-done.3.next_sib_ref = bf16[256,768]{1,0:T(8,128)(2,1)S(1)} collective-permute-done((bf16[256,768]{1,0:T(8,128)(2,1)S(1)}, bf16[256,768]{1,0:T(8,128)(2,1)S(1)}, u32[]{:S(2)}, u32[]{:S(2)}) %collective-permute-start.3) | collective-permute-done | bytes 393248 | tf_op jit(solution)/shard_map/ppermute | solution.py:70
  62.3 0.0 copy-done
  62.3 1.7 %shard_map.28 = f32[128,1,4]{2,1,0:T(1,128)S(1)} custom-call(s32[2]{0:T(128)S(1)} %pad_add_fusion.place_ref, s32[64,64]{1,0:T(8,128)S(1)} %copy-done, bf16[256,768]{1,0:T(8,128)(2,1)S(1)} %bitcast.16, bf16[256,768]{1,0:T(8,128)(2,1)S(1)} %collective-permute-done.sib_ref, bf16[256,768]{1,0:T(8,128)(2,1)S(1)} %collective-permute-done.1.cross_ref, ...), custom_call_target="tpu_custom_call" | custom-call | flops 805306368 | bytes 1966080 | tf_op jit(solution)/shard_map/pallas_call | solution.py:56
  64.0 26.6 %all_to_all.11 = f32[128,1,4]{2,1,0:T(1,128)S(1)} all-to-all(f32[128,1,4]{2,1,0:T(1,128)S(1)} %shard_map.28), channel_id=1, replica_groups={{0,8,16,24,32,40,48,56,64,72,80,88,96,104,112,120,128,136,144,152,160,1..., dimensions={0} | all-to-all | bytes 4096 | tf_op jit(solution)/shard_map/all_to_all | solution.py:96
  90.7 0.7 copy.5
  (3 shorter events, 0.1 us)
Async XLA Ops:
  0.0 1.4 %copy-start.1 = (bf16[1,4,64,768]{3,2,1,0:T(8,128)(2,1)S(1)}, bf16[1,4,64,768]{3,2,1,0:T(8,128)(2,1)}, u32[]{:S(2)}) copy-start(bf16[1,4,64,768]{3,2,1,0:T(8,128)(2,1)} %param.2) | copy-start | bytes 1179652
  45.6 16.7 %copy-start = (s32[64,64]{1,0:T(8,128)S(1)}, s32[64,64]{1,0:T(8,128)}, u32[]{:S(2)}) copy-start(s32[64,64]{1,0:T(8,128)} %counts_ref.1) | copy-start | bytes 49156
  45.7 12.9 %collective-permute-start.2 = (bf16[256,768]{1,0:T(8,128)(2,1)S(1)}, bf16[256,768]{1,0:T(8,128)(2,1)S(1)}, u32[]{:S(2)}, u32[]{:S(2)}) collective-permute-start(bf16[256,768]{1,0:T(8,128)(2,1)S(1)} %bitcast.13), channel_id=1, source_target_pairs={{0,2},{1,3},{2,0},{3,1},{4,6},{5,7},{6,4},{7,5},{8,10},{9,11},{10,... | collective-permute-start | bytes 1179656 | tf_op jit(solution)/shard_map/ppermute | solution.py:70
  48.9 12.2 %collective-permute-start.1 = (bf16[256,768]{1,0:T(8,128)(2,1)S(1)}, bf16[256,768]{1,0:T(8,128)(2,1)S(1)}, u32[]{:S(2)}, u32[]{:S(2)}) collective-permute-start(bf16[256,768]{1,0:T(8,128)(2,1)S(1)} %bitcast.14), channel_id=1, source_target_pairs={{0,6},{1,7},{2,4},{3,5},{4,2},{5,3},{6,0},{7,1},{8,14},{9,15},{10,... | collective-permute-start | bytes 1179656 | tf_op jit(solution)/shard_map/ppermute | solution.py:70
  52.7 8.4 %collective-permute-start = (bf16[256,768]{1,0:T(8,128)(2,1)S(1)}, bf16[256,768]{1,0:T(8,128)(2,1)S(1)}, u32[]{:S(2)}, u32[]{:S(2)}) collective-permute-start(bf16[256,768]{1,0:T(8,128)(2,1)S(1)} %bitcast.15), channel_id=1, source_target_pairs={{0,1},{1,0},{2,3},{3,2},{4,5},{5,4},{6,7},{7,6},{8,9},{9,8},{10,11... | collective-permute-start | bytes 1179656 | tf_op jit(solution)/shard_map/ppermute | solution.py:70
  58.5 3.8 %collective-permute-start.3 = (bf16[256,768]{1,0:T(8,128)(2,1)S(1)}, bf16[256,768]{1,0:T(8,128)(2,1)S(1)}, u32[]{:S(2)}, u32[]{:S(2)}) collective-permute-start(bf16[256,768]{1,0:T(8,128)(2,1)S(1)} %collective-permute-done.2.next_ref), channel_id=1, source_target_pairs={{0,1},{1,0},{2,3},{3,2},{4,5},{5,4},{6,7},{7,6},{8,9},{9,8},{10,11... | collective-permute-start | bytes 1179656 | tf_op jit(solution)/shard_map/ppermute | solution.py:70

commit v4 on v3

--- a/solution.py
+++ b/solution.py
@@ -8,10 +8,10 @@
 EPS = 1e-06
 FAR = 1 << 20
 LANES = 128
-CORE, NEXT, CROSS = 1, 2, 6
+CORE, NEXT, CROSS = 1, 6, 2
 
 
-def nearest_kernel(place_ref, counts_ref, own_ref, sib_ref, cross_ref, next_ref, next_sib_ref, out_ref):
+def nearest_kernel(place_ref, counts_ref, own_ref, chip_ref, cross_ref, next_ref, out_ref):
     cluster, member = place_ref[0], place_ref[1]
     rows = own_ref.shape[0]
     groups = counts_ref.shape[0]
@@ -25,17 +25,18 @@
     row = lax.broadcasted_iota(jnp.int32, (rows, 1), 0)
 
     keys = []
-    for key_ref, mask in ((own_ref, 0), (sib_ref, CORE), (next_ref, NEXT), (next_sib_ref, NEXT ^ CORE)):
-        start = (member ^ mask) * rows
-        slot = (start + lane) // groups
-        keys.append((key_ref, jnp.where(slot < sizes, start + lane, FAR)))
+    for keys_ref, first in ((chip_ref, member & ~CORE), (next_ref, (member ^ NEXT) & ~CORE)):
+        for core in range(2):
+            start = (first + core) * rows
+            slot = (start + lane) // groups
+            keys.append((keys_ref, core, jnp.where(slot < sizes, start + lane, FAR)))
     results = []
     for query_ref, mask in ((own_ref, 0), (cross_ref, CROSS)):
         query_pos = (member ^ mask) * rows + row
         best = jnp.full((rows, LANES), -1.0, jnp.float32)
-        for key_ref, key_pos in keys:
+        for keys_ref, core, key_pos in keys:
             score = lax.dot_general(
-                query_ref[...], key_ref[...], (((1,), (1,)), ((), ())), preferred_element_type=jnp.float32
+                query_ref[...], keys_ref[core], (((1,), (1,)), ((), ())), preferred_element_type=jnp.float32
             )
             score = jnp.where(key_pos < query_pos, score, -1.0)
             for first in range(0, rows, LANES):
@@ -49,25 +50,29 @@
     out_ref[groups:, 0, :] = jnp.where(own_low, results[1], results[0])
 
 
-def nearest_of(place, counts, own, cross, sib, nxt, next_sib):
+def nearest_of(place, counts, own, chip, cross, nxt):
     rows, width = own.shape
     groups = counts.shape[0]
     vmem = pl.BlockSpec(memory_space=pltpu.VMEM)
     return pl.pallas_call(
         nearest_kernel,
         out_shape=jax.ShapeDtypeStruct((2 * groups, 1, rows // groups), jnp.float32),
-        in_specs=[pl.BlockSpec(memory_space=pltpu.SMEM)] + [vmem] * 6,
+        in_specs=[pl.BlockSpec(memory_space=pltpu.SMEM)] + [vmem] * 5,
         out_specs=vmem,
         compiler_params=pltpu.CompilerParams(vmem_limit_bytes=32 << 20),
         cost_estimate=pl.CostEstimate(
             flops=16 * rows * rows * width, bytes_accessed=10 * rows * width, transcendentals=0
         ),
-    )(place, counts, own, sib, cross, nxt, next_sib)
+    )(place, counts, own, chip, cross, nxt)
 
 
 def make_on_device(clusters, members):
     def trade(array, mask):
         return lax.ppermute(array, "mem", [(m, m ^ mask) for m in range(members)])
+
+    def both_cores(array):
+        chips = [[m, m ^ CORE] for m in range(0, members, 2)]
+        return lax.all_gather(array, "mem", axis=0, axis_index_groups=chips)
 
     lows = [m for m in range(members) if m < m ^ CROSS]
     returns = [
@@ -89,10 +94,10 @@
         rows = owned.reshape(slot_dev * groups, width)
         next_rows = trade(rows, NEXT)
         cross_rows = trade(rows, CROSS)
-        sib_rows = trade(rows, CORE)
-        next_sib_rows = trade(next_rows, CORE)
+        chip_rows = both_cores(rows)
+        next_chip_rows = both_cores(next_rows)
         place = jnp.stack([cluster, member]).astype(jnp.int32)
-        best = nearest_of(place, counts, rows, cross_rows, sib_rows, next_rows, next_sib_rows)
+        best = nearest_of(place, counts, rows, chip_rows, cross_rows, next_chip_rows)
         back = lax.all_to_all(
             best, ("grp", "mem"), split_axis=0, concat_axis=0, tiled=True, axis_index_groups=returns
         )

time: 91.6 us -> 89.1 us (0.973)
  the two profiles are of different devices: /device:TPU:1 before, /device:TPU:24 now
where the time goes in v4:
time: 89.1 us; the launch traced here: 87.7 us
  blocking collectives  74.6 us (84%)
  starting transfers between devices  5 us (6%)
  waiting for transfers between devices  3.81 us (4%)
  other arithmetic  1.86 us (2%)
  Pallas kernels  1.66 us (2%)
    all_to_all x1, blocking collectives, on_device(): lax.all_to_all(units, 'grp', split_axis=1, concat_axis=1, tiled=True)  45.7 us
    all_to_all x1, blocking collectives, on_device(): lax.all_to_all(best, ('grp', 'mem'), split_axis=0, concat_axis=0, tiled=T...  24.2 us
    ppermute x2, starting transfers between devices, trade(): return lax.ppermute(array, 'mem', [(m, m ^ mask) for m in range(members)])  5 us
    all_gather x2, blocking collectives, both_cores(): return lax.all_gather(array, 'mem', axis=0, axis_index_groups=chips)  4.73 us
    ppermute x2, waiting for transfers between devices, trade(): return lax.ppermute(array, 'mem', [(m, m ^ mask) for m in range(members)])  3.81 us
  transfers between devices with their start and end apart: 2, of which 1 were waited for; matrix products, arithmetic and copies ran while one was open for 0% of the time, Pallas kernels for 0%

profile of v4, /device:TPU:24, one launch (start us, length us, event | category | flops | bytes accessed | tf_op | source)
XLA Modules:
  0.0 87.7 jit_solution(11641314425018605041)
XLA Ops:
  0.0 0.0 copy-start.1
  0.0 1.4 %fusion = f32[4,64]{0,1:T(8,128)S(1)} fusion(bf16[1,4,64,768]{3,2,1,0:T(8,128)(2,1)} %param.2), kind=kLoop, calls=%fused_computation.2 | loop fusion | flops 589568 | bytes 394240 | tf_op jit(solution)/shard_map/reduce_sum | solution.py:91
  1.4 0.0 copy-done.1
  1.5 0.3 fusion.1
  1.8 45.7 %all_to_all.10 = bf16[4,64,768]{2,0,1:T(4,128)(2,1)S(1)} all-to-all(bf16[4,64,768]{2,0,1:T(4,128)(2,1)S(1)} %fusion.1), channel_id=1, replica_groups=mesh['grp'=64,'mem'=8] {'grp'}, dimensions={1} | all-to-all | bytes 786432 | tf_op jit(solution)/shard_map/all_to_all | solution.py:93
  47.5 2.1 %collective-permute-start.1 = (bf16[256,768]{1,0:T(8,128)(2,1)S(1)}, bf16[256,768]{1,0:T(8,128)(2,1)S(1)}, u32[]{:S(2)}, u32[]{:S(2)}) collective-permute-start(bf16[256,768]{1,0:T(8,128)(2,1)S(1)} %bitcast.15), channel_id=1, source_target_pairs={{0,6},{1,7},{2,4},{3,5},{4,2},{5,3},{6,0},{7,1},{8,14},{9,15},{10,... | collective-permute-start | bytes 1179656 | tf_op jit(solution)/shard_map/ppermute | solution.py:71
  49.7 0.1 pad_add_fusion.place_ref
  49.7 2.9 %collective-permute-start = (bf16[256,768]{1,0:T(8,128)(2,1)S(1)}, bf16[256,768]{1,0:T(8,128)(2,1)S(1)}, u32[]{:S(2)}, u32[]{:S(2)}) collective-permute-start(bf16[256,768]{1,0:T(8,128)(2,1)S(1)} %bitcast.16), channel_id=1, source_target_pairs={{0,2},{1,3},{2,0},{3,1},{4,6},{5,7},{6,4},{7,5},{8,10},{9,11},{10,... | collective-permute-start | bytes 1179656 | tf_op jit(solution)/shard_map/ppermute | solution.py:71
  52.6 2.4 %all_gather.9.chip_ref = bf16[2,256,768]{2,1,0:T(8,128)(2,1)S(1)} all-gather(bf16[1,256,768]{2,1,0:T(8,128)(2,1)S(1)} %bitcast.17), channel_id=1, replica_groups={{0,1},{2,3},{4,5},{6,7},{8,9},{10,11},{12,13},{14,15},{16,17},{18,19},{..., dimensions={0}, use_global_device_ids=true | all-gather | bytes 1179648 | tf_op jit(solution)/shard_map/all_gather | solution.py:75
  55.0 0.0 copy-start
  55.0 3.8 %collective-permute-done.1 = bf16[256,768]{1,0:T(8,128)(2,1)S(1)} collective-permute-done((bf16[256,768]{1,0:T(8,128)(2,1)S(1)}, bf16[256,768]{1,0:T(8,128)(2,1)S(1)}, u32[]{:S(2)}, u32[]{:S(2)}) %collective-permute-start.1) | collective-permute-done | bytes 393248 | tf_op jit(solution)/shard_map/ppermute | solution.py:71
  58.8 2.4 %all-gather = bf16[512,768]{1,0:T(8,128)(2,1)S(1)} all-gather(bf16[256,768]{1,0:T(8,128)(2,1)S(1)} %collective-permute-done.1), channel_id=2, replica_groups={{0,1},{2,3},{4,5},{6,7},{8,9},{10,11},{12,13},{14,15},{16,17},{18,19},{..., dimensions={0}, use_global_device_ids=true | all-gather | bytes 1179648 | tf_op jit(solution)/shard_map/all_gather | solution.py:75
  61.2 0.0 collective-permute-done.cross_ref
  61.2 0.0 copy-done
  61.2 1.7 %shard_map.28 = f32[128,1,4]{2,1,0:T(1,128)S(1)} custom-call(s32[2]{0:T(128)S(1)} %pad_add_fusion.place_ref, s32[64,64]{1,0:T(8,128)S(1)} %copy-done, bf16[256,768]{1,0:T(8,128)(2,1)S(1)} %bitcast.18, bf16[2,256,768]{2,1,0:T(8,128)(2,1)S(1)} %all_gather.9.chip_ref, bf16[256,768]{1,0:T(8,128)(2,1)S(1)} %collective-permute-done.cross_ref, ...), custom_call_target="tpu_custom_call" | custom-call | flops 805306368 | bytes 1966080 | tf_op jit(solution)/shard_map/pallas_call | solution.py:57
  62.8 24.2 %all_to_all.11 = f32[128,1,4]{2,1,0:T(1,128)S(1)} all-to-all(f32[128,1,4]{2,1,0:T(1,128)S(1)} %shard_map.28), channel_id=1, replica_groups={{0,8,16,24,32,40,48,56,64,72,80,88,96,104,112,120,128,136,144,152,160,1..., dimensions={0} | all-to-all | bytes 4096 | tf_op jit(solution)/shard_map/all_to_all | solution.py:101
  87.1 0.7 copy.9
  (3 shorter events, 0.1 us)
Async XLA Ops:
  0.0 1.4 %copy-start.1 = (bf16[1,4,64,768]{3,2,1,0:T(8,128)(2,1)S(1)}, bf16[1,4,64,768]{3,2,1,0:T(8,128)(2,1)}, u32[]{:S(2)}) copy-start(bf16[1,4,64,768]{3,2,1,0:T(8,128)(2,1)} %param.2) | copy-start | bytes 1179652
  47.5 11.3 %collective-permute-start.1 = (bf16[256,768]{1,0:T(8,128)(2,1)S(1)}, bf16[256,768]{1,0:T(8,128)(2,1)S(1)}, u32[]{:S(2)}, u32[]{:S(2)}) collective-permute-start(bf16[256,768]{1,0:T(8,128)(2,1)S(1)} %bitcast.15), channel_id=1, source_target_pairs={{0,6},{1,7},{2,4},{3,5},{4,2},{5,3},{6,0},{7,1},{8,14},{9,15},{10,... | collective-permute-start | bytes 1179656 | tf_op jit(solution)/shard_map/ppermute | solution.py:71
  49.7 11.4 %collective-permute-start = (bf16[256,768]{1,0:T(8,128)(2,1)S(1)}, bf16[256,768]{1,0:T(8,128)(2,1)S(1)}, u32[]{:S(2)}, u32[]{:S(2)}) collective-permute-start(bf16[256,768]{1,0:T(8,128)(2,1)S(1)} %bitcast.16), channel_id=1, source_target_pairs={{0,2},{1,3},{2,0},{3,1},{4,6},{5,7},{6,4},{7,5},{8,10},{9,11},{10,... | collective-permute-start | bytes 1179656 | tf_op jit(solution)/shard_map/ppermute | solution.py:71
  55.0 6.2 %copy-start = (s32[64,64]{1,0:T(8,128)S(1)}, s32[64,64]{1,0:T(8,128)}, u32[]{:S(2)}) copy-start(s32[64,64]{1,0:T(8,128)} %counts_ref.1) | copy-start | bytes 49156

commit v5 on v4

--- a/solution.py
+++ b/solution.py
@@ -9,6 +9,7 @@
 FAR = 1 << 20
 LANES = 128
 CORE, NEXT, CROSS = 1, 6, 2
+FLIP = 63
 
 
 def nearest_kernel(place_ref, counts_ref, own_ref, chip_ref, cross_ref, next_ref, out_ref):
@@ -18,11 +19,12 @@
     slots = rows // groups
     column = lax.broadcasted_iota(jnp.int32, counts_ref.shape, 1)
     sizes = jnp.sum(jnp.where(column == cluster, counts_ref[...], 0), axis=1, keepdims=True)
-    sizes = jnp.broadcast_to(sizes.astype(jnp.float32), (groups, LANES))
-    sizes = jnp.transpose(sizes)[0:1, :].astype(jnp.int32)
+    source = lax.broadcasted_iota(jnp.int32, (groups, groups), 0)
+    place = lax.broadcasted_iota(jnp.int32, (groups, groups), 1)
+    sizes = jnp.sum(jnp.where(source == place ^ FLIP, sizes, 0), axis=0, keepdims=True)
     sizes = jnp.concatenate([sizes] * slots, axis=1)
-    lane = lax.broadcasted_iota(jnp.int32, (1, rows), 1)
-    row = lax.broadcasted_iota(jnp.int32, (rows, 1), 0)
+    lane = lax.broadcasted_iota(jnp.int32, (1, rows), 1) ^ FLIP
+    row = lax.broadcasted_iota(jnp.int32, (rows, 1), 0) ^ FLIP
 
     keys = []
     for keys_ref, first in ((chip_ref, member & ~CORE), (next_ref, (member ^ NEXT) & ~CORE)):
@@ -74,13 +76,15 @@
         chips = [[m, m ^ CORE] for m in range(0, members, 2)]
         return lax.all_gather(array, "mem", axis=0, axis_index_groups=chips)
 
+    owners = [c ^ FLIP for c in range(clusters)]
+    sends = [[c * members + m for c in owners] for m in range(members)]
     lows = [m for m in range(members) if m < m ^ CROSS]
     returns = [
-        [c * members + m for m in (low, low ^ CROSS) for c in range(clusters)] for low in lows
+        [c * members + m for m in (low, low ^ CROSS) for c in owners] for low in lows
     ]
 
     def on_device(embeddings, counts):
-        cluster = lax.axis_index("grp")
+        cluster = lax.axis_index("grp") ^ FLIP
         member = lax.axis_index("mem")
         slot_dev = embeddings.shape[1]
         groups = embeddings.shape[2]
@@ -90,7 +94,9 @@
         units = (
             values * lax.rsqrt(jnp.sum(values * values, axis=-1, keepdims=True) + EPS)
         ).astype(jnp.bfloat16)
-        owned = lax.all_to_all(units, "grp", split_axis=1, concat_axis=1, tiled=True)
+        owned = lax.all_to_all(
+            units, ("grp", "mem"), split_axis=1, concat_axis=1, tiled=True, axis_index_groups=sends
+        )
         rows = owned.reshape(slot_dev * groups, width)
         next_rows = trade(rows, NEXT)
         cross_rows = trade(rows, CROSS)

time: 89.1 us -> 85.6 us (0.961)
  blocking collectives: 74.6 us -> 71.9 us
    all_to_all x1, blocking collectives: 45.7 us -> 43 us  [on_device(): lax.all_to_all(units, ('grp', 'mem'), split_axis=1, concat_axis=1, tiled=...]
where the time goes in v5:
time: 85.6 us; the launch traced here: 84.8 us
  blocking collectives  71.9 us (84%)
  starting transfers between devices  5 us (6%)
  waiting for transfers between devices  3.56 us (4%)
  other arithmetic  1.86 us (2%)
  Pallas kernels  1.66 us (2%)
    all_to_all x1, blocking collectives, on_device(): lax.all_to_all(units, ('grp', 'mem'), split_axis=1, concat_axis=1, tiled=...  43 us
    all_to_all x1, blocking collectives, on_device(): lax.all_to_all(best, ('grp', 'mem'), split_axis=0, concat_axis=0, tiled=T...  24.2 us
    ppermute x2, starting transfers between devices, trade(): return lax.ppermute(array, 'mem', [(m, m ^ mask) for m in range(members)])  5 us
    all_gather x2, blocking collectives, both_cores(): return lax.all_gather(array, 'mem', axis=0, axis_index_groups=chips)  4.73 us
    ppermute x2, waiting for transfers between devices, trade(): return lax.ppermute(array, 'mem', [(m, m ^ mask) for m in range(members)])  3.56 us
  transfers between devices with their start and end apart: 2, of which 1 were waited for; matrix products, arithmetic and copies ran while one was open for 0% of the time, Pallas kernels for 0%

profile of v5, /device:TPU:24, one launch (start us, length us, event | category | flops | bytes accessed | tf_op | source)
XLA Modules:
  0.0 84.8 jit_solution(8836031260142789997)
XLA Ops:
  0.0 0.0 copy-start.1
  0.0 1.4 %fusion = f32[4,64]{0,1:T(8,128)S(1)} fusion(bf16[1,4,64,768]{3,2,1,0:T(8,128)(2,1)} %param.2), kind=kLoop, calls=%fused_computation.2 | loop fusion | flops 589568 | bytes 394240 | tf_op jit(solution)/shard_map/reduce_sum | solution.py:95
  1.4 0.0 copy-done.1
  1.5 0.3 fusion.1
  1.8 43.0 %all_to_all.10 = bf16[4,64,768]{2,0,1:T(4,128)(2,1)S(1)} all-to-all(bf16[4,64,768]{2,0,1:T(4,128)(2,1)S(1)} %fusion.1), channel_id=1, replica_groups={{504,496,488,480,472,464,456,448,440,432,424,416,408,400,392,384,376,36..., dimensions={1} | all-to-all | bytes 786432 | tf_op jit(solution)/shard_map/all_to_all | solution.py:97
  44.9 2.1 %collective-permute-start.1 = (bf16[256,768]{1,0:T(8,128)(2,1)S(1)}, bf16[256,768]{1,0:T(8,128)(2,1)S(1)}, u32[]{:S(2)}, u32[]{:S(2)}) collective-permute-start(bf16[256,768]{1,0:T(8,128)(2,1)S(1)} %bitcast.15), channel_id=1, source_target_pairs={{0,6},{1,7},{2,4},{3,5},{4,2},{5,3},{6,0},{7,1},{8,14},{9,15},{10,... | collective-permute-start | bytes 1179656 | tf_op jit(solution)/shard_map/ppermute | solution.py:73
  47.0 0.1 pad_add_fusion.place_ref
  47.1 2.9 %collective-permute-start = (bf16[256,768]{1,0:T(8,128)(2,1)S(1)}, bf16[256,768]{1,0:T(8,128)(2,1)S(1)}, u32[]{:S(2)}, u32[]{:S(2)}) collective-permute-start(bf16[256,768]{1,0:T(8,128)(2,1)S(1)} %bitcast.16), channel_id=1, source_target_pairs={{0,2},{1,3},{2,0},{3,1},{4,6},{5,7},{6,4},{7,5},{8,10},{9,11},{10,... | collective-permute-start | bytes 1179656 | tf_op jit(solution)/shard_map/ppermute | solution.py:73
  50.0 2.4 %all_gather.9.chip_ref = bf16[2,256,768]{2,1,0:T(8,128)(2,1)S(1)} all-gather(bf16[1,256,768]{2,1,0:T(8,128)(2,1)S(1)} %bitcast.17), channel_id=1, replica_groups={{0,1},{2,3},{4,5},{6,7},{8,9},{10,11},{12,13},{14,15},{16,17},{18,19},{..., dimensions={0}, use_global_device_ids=true | all-gather | bytes 1179648 | tf_op jit(solution)/shard_map/all_gather | solution.py:77
  52.3 0.0 copy-start
  52.3 3.6 %collective-permute-done.1 = bf16[256,768]{1,0:T(8,128)(2,1)S(1)} collective-permute-done((bf16[256,768]{1,0:T(8,128)(2,1)S(1)}, bf16[256,768]{1,0:T(8,128)(2,1)S(1)}, u32[]{:S(2)}, u32[]{:S(2)}) %collective-permute-start.1) | collective-permute-done | bytes 393248 | tf_op jit(solution)/shard_map/ppermute | solution.py:73
  55.9 2.4 %all-gather = bf16[512,768]{1,0:T(8,128)(2,1)S(1)} all-gather(bf16[256,768]{1,0:T(8,128)(2,1)S(1)} %collective-permute-done.1), channel_id=2, replica_groups={{0,1},{2,3},{4,5},{6,7},{8,9},{10,11},{12,13},{14,15},{16,17},{18,19},{..., dimensions={0}, use_global_device_ids=true | all-gather | bytes 1179648 | tf_op jit(solution)/shard_map/all_gather | solution.py:77
  58.3 0.0 collective-permute-done.cross_ref
  58.3 0.0 copy-done
  58.3 1.7 %shard_map.28 = f32[128,1,4]{2,1,0:T(1,128)S(1)} custom-call(s32[2]{0:T(128)S(1)} %pad_add_fusion.place_ref, s32[64,64]{1,0:T(8,128)S(1)} %copy-done, bf16[256,768]{1,0:T(8,128)(2,1)S(1)} %bitcast.18, bf16[2,256,768]{2,1,0:T(8,128)(2,1)S(1)} %all_gather.9.chip_ref, bf16[256,768]{1,0:T(8,128)(2,1)S(1)} %collective-permute-done.cross_ref, ...), custom_call_target="tpu_custom_call" | custom-call | flops 805306368 | bytes 1966080 | tf_op jit(solution)/shard_map/pallas_call | solution.py:59
  59.9 24.2 %all_to_all.11 = f32[128,1,4]{2,1,0:T(1,128)S(1)} all-to-all(f32[128,1,4]{2,1,0:T(1,128)S(1)} %shard_map.28), channel_id=1, replica_groups={{504,496,488,480,472,464,456,448,440,432,424,416,408,400,392,384,376,36..., dimensions={0} | all-to-all | bytes 4096 | tf_op jit(solution)/shard_map/all_to_all | solution.py:107
  84.1 0.7 copy.9
  (3 shorter events, 0.1 us)
Async XLA Ops:
  0.0 1.4 %copy-start.1 = (bf16[1,4,64,768]{3,2,1,0:T(8,128)(2,1)S(1)}, bf16[1,4,64,768]{3,2,1,0:T(8,128)(2,1)}, u32[]{:S(2)}) copy-start(bf16[1,4,64,768]{3,2,1,0:T(8,128)(2,1)} %param.2) | copy-start | bytes 1179652
  44.9 11.0 %collective-permute-start.1 = (bf16[256,768]{1,0:T(8,128)(2,1)S(1)}, bf16[256,768]{1,0:T(8,128)(2,1)S(1)}, u32[]{:S(2)}, u32[]{:S(2)}) collective-permute-start(bf16[256,768]{1,0:T(8,128)(2,1)S(1)} %bitcast.15), channel_id=1, source_target_pairs={{0,6},{1,7},{2,4},{3,5},{4,2},{5,3},{6,0},{7,1},{8,14},{9,15},{10,... | collective-permute-start | bytes 1179656 | tf_op jit(solution)/shard_map/ppermute | solution.py:73
  47.1 11.2 %collective-permute-start = (bf16[256,768]{1,0:T(8,128)(2,1)S(1)}, bf16[256,768]{1,0:T(8,128)(2,1)S(1)}, u32[]{:S(2)}, u32[]{:S(2)}) collective-permute-start(bf16[256,768]{1,0:T(8,128)(2,1)S(1)} %bitcast.16), channel_id=1, source_target_pairs={{0,2},{1,3},{2,0},{3,1},{4,6},{5,7},{6,4},{7,5},{8,10},{9,11},{10,... | collective-permute-start | bytes 1179656 | tf_op jit(solution)/shard_map/ppermute | solution.py:73
  52.3 5.9 %copy-start = (s32[64,64]{1,0:T(8,128)S(1)}, s32[64,64]{1,0:T(8,128)}, u32[]{:S(2)}) copy-start(s32[64,64]{1,0:T(8,128)} %counts_ref.1) | copy-start | bytes 49156

commit v6 on v5

--- a/solution.py
+++ b/solution.py
@@ -9,7 +9,15 @@
 FAR = 1 << 20
 LANES = 128
 CORE, NEXT, CROSS = 1, 6, 2
-FLIP = 63
+FAR_HALF, NEAR_HALF = 34, 62
+
+
+def group_at(place, half):
+    return place ^ jnp.where(place % (2 * half) < half, FAR_HALF, NEAR_HALF)
+
+
+def place_of(group, half):
+    return group ^ jnp.where(group < half, NEAR_HALF, FAR_HALF)
 
 
 def nearest_kernel(place_ref, counts_ref, own_ref, chip_ref, cross_ref, next_ref, out_ref):
@@ -21,10 +29,10 @@
     sizes = jnp.sum(jnp.where(column == cluster, counts_ref[...], 0), axis=1, keepdims=True)
     source = lax.broadcasted_iota(jnp.int32, (groups, groups), 0)
     place = lax.broadcasted_iota(jnp.int32, (groups, groups), 1)
-    sizes = jnp.sum(jnp.where(source == place ^ FLIP, sizes, 0), axis=0, keepdims=True)
+    sizes = jnp.sum(jnp.where(source == group_at(place, groups // 2), sizes, 0), axis=0, keepdims=True)
     sizes = jnp.concatenate([sizes] * slots, axis=1)
-    lane = lax.broadcasted_iota(jnp.int32, (1, rows), 1) ^ FLIP
-    row = lax.broadcasted_iota(jnp.int32, (rows, 1), 0) ^ FLIP
+    lane = group_at(lax.broadcasted_iota(jnp.int32, (1, rows), 1), groups // 2)
+    row = group_at(lax.broadcasted_iota(jnp.int32, (rows, 1), 0), groups // 2)
 
     keys = []
     for keys_ref, first in ((chip_ref, member & ~CORE), (next_ref, (member ^ NEXT) & ~CORE)):
@@ -76,7 +84,7 @@
         chips = [[m, m ^ CORE] for m in range(0, members, 2)]
         return lax.all_gather(array, "mem", axis=0, axis_index_groups=chips)
 
-    owners = [c ^ FLIP for c in range(clusters)]
+    owners = [c ^ (FAR_HALF if c < clusters // 2 else NEAR_HALF) for c in range(clusters)]
     sends = [[c * members + m for c in owners] for m in range(members)]
     lows = [m for m in range(members) if m < m ^ CROSS]
     returns = [
@@ -84,7 +92,7 @@
     ]
 
     def on_device(embeddings, counts):
-        cluster = lax.axis_index("grp") ^ FLIP
+        cluster = place_of(lax.axis_index("grp"), clusters // 2)
         member = lax.axis_index("mem")
         slot_dev = embeddings.shape[1]
         groups = embeddings.shape[2]

time: 85.6 us -> 81.8 us (0.956)
  blocking collectives: 71.9 us -> 65.1 us
  waiting for transfers between devices: 3.56 us -> 6.28 us
    all_to_all x1, blocking collectives: 43 us -> 39.6 us  [on_device(): lax.all_to_all(units, ('grp', 'mem'), split_axis=1, concat_axis=1, tiled=...]
    all_to_all x1, blocking collectives: 24.2 us -> 20.8 us  [on_device(): lax.all_to_all(best, ('grp', 'mem'), split_axis=0, concat_axis=0, tiled=T...]
    ppermute x2, waiting for transfers between devices: 3.56 us -> 6.28 us  [trade(): return lax.ppermute(array, 'mem', [(m, m ^ mask) for m in range(members)])]
where the time goes in v6:
time: 81.8 us; the launch traced here: 80.7 us
  blocking collectives  65.1 us (80%)
  waiting for transfers between devices  6.28 us (8%)
  starting transfers between devices  5 us (6%)
  other arithmetic  1.86 us (2%)
  Pallas kernels  1.66 us (2%)
    all_to_all x1, blocking collectives, on_device(): lax.all_to_all(units, ('grp', 'mem'), split_axis=1, concat_axis=1, tiled=...  39.6 us
    all_to_all x1, blocking collectives, on_device(): lax.all_to_all(best, ('grp', 'mem'), split_axis=0, concat_axis=0, tiled=T...  20.8 us
    ppermute x2, waiting for transfers between devices, trade(): return lax.ppermute(array, 'mem', [(m, m ^ mask) for m in range(members)])  6.28 us
    ppermute x2, starting transfers between devices, trade(): return lax.ppermute(array, 'mem', [(m, m ^ mask) for m in range(members)])  5 us
    all_gather x2, blocking collectives, both_cores(): return lax.all_gather(array, 'mem', axis=0, axis_index_groups=chips)  4.73 us
    pallas_call x1, Pallas kernels, nearest_of(): pl.pallas_call(nearest_kernel, out_shape=jax.ShapeDtypeStruct((2 * groups...  1.66 us
  transfers between devices with their start and end apart: 2, of which 1 were waited for; matrix products, arithmetic and copies ran while one was open for 0% of the time, Pallas kernels for 0%

profile of v6, /device:TPU:24, one launch (start us, length us, event | category | flops | bytes accessed | tf_op | source)
XLA Modules:
  0.0 80.7 jit_solution(242477785779848350)
XLA Ops:
  0.0 0.0 copy-start.1
  0.0 1.4 %fusion = f32[4,64]{0,1:T(8,128)S(1)} fusion(bf16[1,4,64,768]{3,2,1,0:T(8,128)(2,1)} %param.2), kind=kLoop, calls=%fused_computation.2 | loop fusion | flops 589568 | bytes 394240 | tf_op jit(solution)/shard_map/reduce_sum | solution.py:103
  1.4 0.0 copy-done.1
  1.5 0.3 fusion.1
  1.8 39.6 %all_to_all.10 = bf16[4,64,768]{2,0,1:T(4,128)(2,1)S(1)} all-to-all(bf16[4,64,768]{2,0,1:T(4,128)(2,1)S(1)} %fusion.1), channel_id=1, replica_groups={{272,280,256,264,304,312,288,296,336,344,320,328,368,376,352,360,400,40..., dimensions={1} | all-to-all | bytes 786432 | tf_op jit(solution)/shard_map/all_to_all | solution.py:105
  41.5 2.1 %collective-permute-start.1 = (bf16[256,768]{1,0:T(8,128)(2,1)S(1)}, bf16[256,768]{1,0:T(8,128)(2,1)S(1)}, u32[]{:S(2)}, u32[]{:S(2)}) collective-permute-start(bf16[256,768]{1,0:T(8,128)(2,1)S(1)} %bitcast.15), channel_id=1, source_target_pairs={{0,6},{1,7},{2,4},{3,5},{4,2},{5,3},{6,0},{7,1},{8,14},{9,15},{10,... | collective-permute-start | bytes 1179656 | tf_op jit(solution)/shard_map/ppermute | solution.py:81
  43.6 0.1 pad_add_fusion.place_ref
  43.7 2.9 %collective-permute-start = (bf16[256,768]{1,0:T(8,128)(2,1)S(1)}, bf16[256,768]{1,0:T(8,128)(2,1)S(1)}, u32[]{:S(2)}, u32[]{:S(2)}) collective-permute-start(bf16[256,768]{1,0:T(8,128)(2,1)S(1)} %bitcast.16), channel_id=1, source_target_pairs={{0,2},{1,3},{2,0},{3,1},{4,6},{5,7},{6,4},{7,5},{8,10},{9,11},{10,... | collective-permute-start | bytes 1179656 | tf_op jit(solution)/shard_map/ppermute | solution.py:81
  46.6 2.4 %all_gather.9.chip_ref = bf16[2,256,768]{2,1,0:T(8,128)(2,1)S(1)} all-gather(bf16[1,256,768]{2,1,0:T(8,128)(2,1)S(1)} %bitcast.17), channel_id=1, replica_groups={{0,1},{2,3},{4,5},{6,7},{8,9},{10,11},{12,13},{14,15},{16,17},{18,19},{..., dimensions={0}, use_global_device_ids=true | all-gather | bytes 1179648 | tf_op jit(solution)/shard_map/all_gather | solution.py:85
  48.9 0.0 copy-start
  48.9 6.3 %collective-permute-done.1 = bf16[256,768]{1,0:T(8,128)(2,1)S(1)} collective-permute-done((bf16[256,768]{1,0:T(8,128)(2,1)S(1)}, bf16[256,768]{1,0:T(8,128)(2,1)S(1)}, u32[]{:S(2)}, u32[]{:S(2)}) %collective-permute-start.1) | collective-permute-done | bytes 393248 | tf_op jit(solution)/shard_map/ppermute | solution.py:81
  55.2 2.4 %all-gather = bf16[512,768]{1,0:T(8,128)(2,1)S(1)} all-gather(bf16[256,768]{1,0:T(8,128)(2,1)S(1)} %collective-permute-done.1), channel_id=2, replica_groups={{0,1},{2,3},{4,5},{6,7},{8,9},{10,11},{12,13},{14,15},{16,17},{18,19},{..., dimensions={0}, use_global_device_ids=true | all-gather | bytes 1179648 | tf_op jit(solution)/shard_map/all_gather | solution.py:85
  57.6 0.0 collective-permute-done.cross_ref
  57.6 0.0 copy-done
  57.6 1.7 %shard_map.28 = f32[128,1,4]{2,1,0:T(1,128)S(1)} custom-call(s32[2]{0:T(128)S(1)} %pad_add_fusion.place_ref, s32[64,64]{1,0:T(8,128)S(1)} %copy-done, bf16[256,768]{1,0:T(8,128)(2,1)S(1)} %bitcast.18, bf16[2,256,768]{2,1,0:T(8,128)(2,1)S(1)} %all_gather.9.chip_ref, bf16[256,768]{1,0:T(8,128)(2,1)S(1)} %collective-permute-done.cross_ref, ...), custom_call_target="tpu_custom_call" | custom-call | flops 805306368 | bytes 1966080 | tf_op jit(solution)/shard_map/pallas_call | solution.py:67
  59.2 20.8 %all_to_all.11 = f32[128,1,4]{2,1,0:T(1,128)S(1)} all-to-all(f32[128,1,4]{2,1,0:T(1,128)S(1)} %shard_map.28), channel_id=1, replica_groups={{272,280,256,264,304,312,288,296,336,344,320,328,368,376,352,360,400,40..., dimensions={0} | all-to-all | bytes 4096 | tf_op jit(solution)/shard_map/all_to_all | solution.py:115
  80.1 0.7 copy.9
  (3 shorter events, 0.1 us)
Async XLA Ops:
  0.0 1.4 %copy-start.1 = (bf16[1,4,64,768]{3,2,1,0:T(8,128)(2,1)S(1)}, bf16[1,4,64,768]{3,2,1,0:T(8,128)(2,1)}, u32[]{:S(2)}) copy-start(bf16[1,4,64,768]{3,2,1,0:T(8,128)(2,1)} %param.2) | copy-start | bytes 1179652
  41.5 13.7 %collective-permute-start.1 = (bf16[256,768]{1,0:T(8,128)(2,1)S(1)}, bf16[256,768]{1,0:T(8,128)(2,1)S(1)}, u32[]{:S(2)}, u32[]{:S(2)}) collective-permute-start(bf16[256,768]{1,0:T(8,128)(2,1)S(1)} %bitcast.15), channel_id=1, source_target_pairs={{0,6},{1,7},{2,4},{3,5},{4,2},{5,3},{6,0},{7,1},{8,14},{9,15},{10,... | collective-permute-start | bytes 1179656 | tf_op jit(solution)/shard_map/ppermute | solution.py:81
  43.7 13.9 %collective-permute-start = (bf16[256,768]{1,0:T(8,128)(2,1)S(1)}, bf16[256,768]{1,0:T(8,128)(2,1)S(1)}, u32[]{:S(2)}, u32[]{:S(2)}) collective-permute-start(bf16[256,768]{1,0:T(8,128)(2,1)S(1)} %bitcast.16), channel_id=1, source_target_pairs={{0,2},{1,3},{2,0},{3,1},{4,6},{5,7},{6,4},{7,5},{8,10},{9,11},{10,... | collective-permute-start | bytes 1179656 | tf_op jit(solution)/shard_map/ppermute | solution.py:81
  48.9 8.6 %copy-start = (s32[64,64]{1,0:T(8,128)S(1)}, s32[64,64]{1,0:T(8,128)}, u32[]{:S(2)}) copy-start(s32[64,64]{1,0:T(8,128)} %counts_ref.1) | copy-start | bytes 49156

commit v7 on v5

--- a/solution.py
+++ b/solution.py
@@ -9,22 +9,33 @@
 FAR = 1 << 20
 LANES = 128
 CORE, NEXT, CROSS = 1, 6, 2
-FLIP = 63
+PLANES = (8, 4, 12, 7, 9, 3, 13, 6, 10, 2, 14, 5, 11, 1, 15, 0)
+LINES = (2, 1, 3, 0)
+ORDER = [plane * len(LINES) + line for plane in PLANES for line in LINES]
+
+
+def group_at(place):
+    plane, line = jnp.zeros_like(place), jnp.zeros_like(place)
+    for index, value in enumerate(PLANES):
+        plane = jnp.where(place // len(LINES) == index, value, plane)
+    for index, value in enumerate(LINES):
+        line = jnp.where(place % len(LINES) == index, value, line)
+    return plane * len(LINES) + line
 
 
 def nearest_kernel(place_ref, counts_ref, own_ref, chip_ref, cross_ref, next_ref, out_ref):
-    cluster, member = place_ref[0], place_ref[1]
+    group, member = place_ref[0], place_ref[1]
     rows = own_ref.shape[0]
     groups = counts_ref.shape[0]
     slots = rows // groups
-    column = lax.broadcasted_iota(jnp.int32, counts_ref.shape, 1)
-    sizes = jnp.sum(jnp.where(column == cluster, counts_ref[...], 0), axis=1, keepdims=True)
+    across = group_at(lax.broadcasted_iota(jnp.int32, (1, groups), 1))
+    down = group_at(lax.broadcasted_iota(jnp.int32, (groups, 1), 0))
+    sizes = jnp.sum(jnp.where(across == group, counts_ref[...], 0), axis=1, keepdims=True)
     source = lax.broadcasted_iota(jnp.int32, (groups, groups), 0)
-    place = lax.broadcasted_iota(jnp.int32, (groups, groups), 1)
-    sizes = jnp.sum(jnp.where(source == place ^ FLIP, sizes, 0), axis=0, keepdims=True)
+    sizes = jnp.sum(jnp.where(source == across, sizes, 0), axis=0, keepdims=True)
     sizes = jnp.concatenate([sizes] * slots, axis=1)
-    lane = lax.broadcasted_iota(jnp.int32, (1, rows), 1) ^ FLIP
-    row = lax.broadcasted_iota(jnp.int32, (rows, 1), 0) ^ FLIP
+    lane = jnp.concatenate([across + t * groups for t in range(slots)], axis=1)
+    row = jnp.concatenate([down + t * groups for t in range(slots)], axis=0)
 
     keys = []
     for keys_ref, first in ((chip_ref, member & ~CORE), (next_ref, (member ^ NEXT) & ~CORE)):
@@ -76,15 +87,13 @@
         chips = [[m, m ^ CORE] for m in range(0, members, 2)]
         return lax.all_gather(array, "mem", axis=0, axis_index_groups=chips)
 
-    owners = [c ^ FLIP for c in range(clusters)]
-    sends = [[c * members + m for c in owners] for m in range(members)]
+    assert sorted(ORDER) == list(range(clusters))
+    sends = [[c * members + m for c in ORDER] for m in range(members)]
     lows = [m for m in range(members) if m < m ^ CROSS]
-    returns = [
-        [c * members + m for m in (low, low ^ CROSS) for c in owners] for low in lows
-    ]
+    returns = [[c * members + m for m in (low, low ^ CROSS) for c in ORDER] for low in lows]
 
     def on_device(embeddings, counts):
-        cluster = lax.axis_index("grp") ^ FLIP
+        group = lax.axis_index("grp")
         member = lax.axis_index("mem")
         slot_dev = embeddings.shape[1]
         groups = embeddings.shape[2]
@@ -102,7 +111,7 @@
         cross_rows = trade(rows, CROSS)
         chip_rows = both_cores(rows)
         next_chip_rows = both_cores(next_rows)
-        place = jnp.stack([cluster, member]).astype(jnp.int32)
+        place = jnp.stack([group, member]).astype(jnp.int32)
         best = nearest_of(place, counts, rows, chip_rows, cross_rows, next_chip_rows)
         back = lax.all_to_all(
             best, ("grp", "mem"), split_axis=0, concat_axis=0, tiled=True, axis_index_groups=returns

time: 85.6 us -> 81.3 us (0.950)
  blocking collectives: 71.9 us -> 64.4 us
  waiting for transfers between devices: 3.56 us -> 6.52 us
    all_to_all x1, blocking collectives: 24.2 us -> 20.2 us  [on_device(): lax.all_to_all(best, ('grp', 'mem'), split_axis=0, concat_axis=0, tiled=T...]
    all_to_all x1, blocking collectives: 43 us -> 39.4 us  [on_device(): lax.all_to_all(units, ('grp', 'mem'), split_axis=1, concat_axis=1, tiled=...]
    ppermute x2, waiting for transfers between devices: 3.56 us -> 6.52 us  [trade(): return lax.ppermute(array, 'mem', [(m, m ^ mask) for m in range(members)])]
where the time goes in v7:
time: 81.3 us; the launch traced here: 80.2 us
  blocking collectives  64.4 us (79%)
  waiting for transfers between devices  6.52 us (8%)
  starting transfers between devices  5 us (6%)
  other arithmetic  1.86 us (2%)
  Pallas kernels  1.67 us (2%)
    all_to_all x1, blocking collectives, on_device(): lax.all_to_all(units, ('grp', 'mem'), split_axis=1, concat_axis=1, tiled=...  39.4 us
    all_to_all x1, blocking collectives, on_device(): lax.all_to_all(best, ('grp', 'mem'), split_axis=0, concat_axis=0, tiled=T...  20.2 us
    ppermute x2, waiting for transfers between devices, trade(): return lax.ppermute(array, 'mem', [(m, m ^ mask) for m in range(members)])  6.52 us
    ppermute x2, starting transfers between devices, trade(): return lax.ppermute(array, 'mem', [(m, m ^ mask) for m in range(members)])  5 us
    all_gather x2, blocking collectives, both_cores(): return lax.all_gather(array, 'mem', axis=0, axis_index_groups=chips)  4.73 us
    pallas_call x1, Pallas kernels, nearest_of(): pl.pallas_call(nearest_kernel, out_shape=jax.ShapeDtypeStruct((2 * groups...  1.67 us
  transfers between devices with their start and end apart: 2, of which 1 were waited for; matrix products, arithmetic and copies ran while one was open for 0% of the time, Pallas kernels for 0%

profile of v7, /device:TPU:24, one launch (start us, length us, event | category | flops | bytes accessed | tf_op | source)
XLA Modules:
  0.0 80.2 jit_solution(3152273298660279161)
XLA Ops:
  0.0 0.0 copy-start.1
  0.0 1.4 %fusion = f32[4,64]{0,1:T(8,128)S(1)} fusion(bf16[1,4,64,768]{3,2,1,0:T(8,128)(2,1)} %param.2), kind=kLoop, calls=%fused_computation.2 | loop fusion | flops 589568 | bytes 394240 | tf_op jit(solution)/shard_map/reduce_sum | solution.py:104
  1.4 0.0 copy-done.1
  1.5 0.3 fusion.1
  1.8 39.4 %all_to_all.10 = bf16[4,64,768]{2,0,1:T(4,128)(2,1)S(1)} all-to-all(bf16[4,64,768]{2,0,1:T(4,128)(2,1)S(1)} %fusion.1), channel_id=1, replica_groups={{272,264,280,256,144,136,152,128,400,392,408,384,240,232,248,224,304,29..., dimensions={1} | all-to-all | bytes 786432 | tf_op jit(solution)/shard_map/all_to_all | solution.py:106
  41.3 2.1 %collective-permute-start.1 = (bf16[256,768]{1,0:T(8,128)(2,1)S(1)}, bf16[256,768]{1,0:T(8,128)(2,1)S(1)}, u32[]{:S(2)}, u32[]{:S(2)}) collective-permute-start(bf16[256,768]{1,0:T(8,128)(2,1)S(1)} %bitcast.15), channel_id=1, source_target_pairs={{0,6},{1,7},{2,4},{3,5},{4,2},{5,3},{6,0},{7,1},{8,14},{9,15},{10,... | collective-permute-start | bytes 1179656 | tf_op jit(solution)/shard_map/ppermute | solution.py:84
  43.4 0.1 pad_add_fusion.place_ref
  43.5 2.9 %collective-permute-start = (bf16[256,768]{1,0:T(8,128)(2,1)S(1)}, bf16[256,768]{1,0:T(8,128)(2,1)S(1)}, u32[]{:S(2)}, u32[]{:S(2)}) collective-permute-start(bf16[256,768]{1,0:T(8,128)(2,1)S(1)} %bitcast.16), channel_id=1, source_target_pairs={{0,2},{1,3},{2,0},{3,1},{4,6},{5,7},{6,4},{7,5},{8,10},{9,11},{10,... | collective-permute-start | bytes 1179656 | tf_op jit(solution)/shard_map/ppermute | solution.py:84
  46.4 2.4 %all_gather.9.chip_ref = bf16[2,256,768]{2,1,0:T(8,128)(2,1)S(1)} all-gather(bf16[1,256,768]{2,1,0:T(8,128)(2,1)S(1)} %bitcast.17), channel_id=1, replica_groups={{0,1},{2,3},{4,5},{6,7},{8,9},{10,11},{12,13},{14,15},{16,17},{18,19},{..., dimensions={0}, use_global_device_ids=true | all-gather | bytes 1179648 | tf_op jit(solution)/shard_map/all_gather | solution.py:88
  48.7 0.0 copy-start
  48.7 6.5 %collective-permute-done.1 = bf16[256,768]{1,0:T(8,128)(2,1)S(1)} collective-permute-done((bf16[256,768]{1,0:T(8,128)(2,1)S(1)}, bf16[256,768]{1,0:T(8,128)(2,1)S(1)}, u32[]{:S(2)}, u32[]{:S(2)}) %collective-permute-start.1) | collective-permute-done | bytes 393248 | tf_op jit(solution)/shard_map/ppermute | solution.py:84
  55.2 2.4 %all-gather = bf16[512,768]{1,0:T(8,128)(2,1)S(1)} all-gather(bf16[256,768]{1,0:T(8,128)(2,1)S(1)} %collective-permute-done.1), channel_id=2, replica_groups={{0,1},{2,3},{4,5},{6,7},{8,9},{10,11},{12,13},{14,15},{16,17},{18,19},{..., dimensions={0}, use_global_device_ids=true | all-gather | bytes 1179648 | tf_op jit(solution)/shard_map/all_gather | solution.py:88
  57.6 0.0 collective-permute-done.cross_ref
  57.6 0.0 copy-done
  57.6 1.7 %shard_map.28 = f32[128,1,4]{2,1,0:T(1,128)S(1)} custom-call(s32[2]{0:T(128)S(1)} %pad_add_fusion.place_ref, s32[64,64]{1,0:T(8,128)S(1)} %copy-done, bf16[256,768]{1,0:T(8,128)(2,1)S(1)} %bitcast.18, bf16[2,256,768]{2,1,0:T(8,128)(2,1)S(1)} %all_gather.9.chip_ref, bf16[256,768]{1,0:T(8,128)(2,1)S(1)} %collective-permute-done.cross_ref, ...), custom_call_target="tpu_custom_call" | custom-call | flops 805306368 | bytes 1966080 | tf_op jit(solution)/shard_map/pallas_call | solution.py:70
  59.3 20.2 %all_to_all.11 = f32[128,1,4]{2,1,0:T(1,128)S(1)} all-to-all(f32[128,1,4]{2,1,0:T(1,128)S(1)} %shard_map.28), channel_id=1, replica_groups={{272,264,280,256,144,136,152,128,400,392,408,384,240,232,248,224,304,29..., dimensions={0} | all-to-all | bytes 4096 | tf_op jit(solution)/shard_map/all_to_all | solution.py:116
  79.5 0.7 copy.9
  (3 shorter events, 0.1 us)
Async XLA Ops:
  0.0 1.4 %copy-start.1 = (bf16[1,4,64,768]{3,2,1,0:T(8,128)(2,1)S(1)}, bf16[1,4,64,768]{3,2,1,0:T(8,128)(2,1)}, u32[]{:S(2)}) copy-start(bf16[1,4,64,768]{3,2,1,0:T(8,128)(2,1)} %param.2) | copy-start | bytes 1179652
  41.3 14.0 %collective-permute-start.1 = (bf16[256,768]{1,0:T(8,128)(2,1)S(1)}, bf16[256,768]{1,0:T(8,128)(2,1)S(1)}, u32[]{:S(2)}, u32[]{:S(2)}) collective-permute-start(bf16[256,768]{1,0:T(8,128)(2,1)S(1)} %bitcast.15), channel_id=1, source_target_pairs={{0,6},{1,7},{2,4},{3,5},{4,2},{5,3},{6,0},{7,1},{8,14},{9,15},{10,... | collective-permute-start | bytes 1179656 | tf_op jit(solution)/shard_map/ppermute | solution.py:84
  43.5 14.1 %collective-permute-start = (bf16[256,768]{1,0:T(8,128)(2,1)S(1)}, bf16[256,768]{1,0:T(8,128)(2,1)S(1)}, u32[]{:S(2)}, u32[]{:S(2)}) collective-permute-start(bf16[256,768]{1,0:T(8,128)(2,1)S(1)} %bitcast.16), channel_id=1, source_target_pairs={{0,2},{1,3},{2,0},{3,1},{4,6},{5,7},{6,4},{7,5},{8,10},{9,11},{10,... | collective-permute-start | bytes 1179656 | tf_op jit(solution)/shard_map/ppermute | solution.py:84
  48.7 8.9 %copy-start = (s32[64,64]{1,0:T(8,128)S(1)}, s32[64,64]{1,0:T(8,128)}, u32[]{:S(2)}) copy-start(s32[64,64]{1,0:T(8,128)} %counts_ref.1) | copy-start | bytes 49156

commit v8 on v7

--- a/solution.py
+++ b/solution.py
@@ -8,6 +8,7 @@
 EPS = 1e-06
 FAR = 1 << 20
 LANES = 128
+LOAD = 16
 CORE, NEXT, CROSS = 1, 6, 2
 PLANES = (8, 4, 12, 7, 9, 3, 13, 6, 10, 2, 14, 5, 11, 1, 15, 0)
 LINES = (2, 1, 3, 0)
@@ -21,6 +22,42 @@
     for index, value in enumerate(LINES):
         line = jnp.where(place % len(LINES) == index, value, line)
     return plane * len(LINES) + line
+
+
+def unit_kernel(items_ref, units_ref, stage_ref, sems):
+    steps, _, rows, _ = stage_ref.shape
+
+    def load(step):
+        part = pl.ds(step * rows, rows)
+        return pltpu.make_async_copy(items_ref.at[0, :, part], stage_ref.at[step], sems.at[step])
+
+    for step in range(steps):
+        load(step).start()
+    for step in range(steps):
+        load(step).wait()
+        values = stage_ref[step].astype(jnp.float32)
+        total = jnp.sum(values * values, axis=-1, keepdims=True)
+        units = values * lax.rsqrt(total + EPS)
+        units_ref[step * rows : (step + 1) * rows] = jnp.transpose(units, (1, 0, 2)).astype(jnp.bfloat16)
+
+
+def units_by_cluster(embeddings):
+    _, slots, clusters, width = embeddings.shape
+    size = slots * clusters * width
+    return pl.pallas_call(
+        unit_kernel,
+        out_shape=jax.ShapeDtypeStruct((clusters, slots, width), jnp.bfloat16),
+        in_specs=[pl.BlockSpec(memory_space=pltpu.HBM)],
+        out_specs=pl.BlockSpec(memory_space=pltpu.VMEM),
+        scratch_shapes=[
+            pltpu.VMEM((clusters // LOAD, slots, LOAD, width), jnp.bfloat16),
+            pltpu.SemaphoreType.DMA((clusters // LOAD,)),
+        ],
+        compiler_params=pltpu.CompilerParams(vmem_limit_bytes=107 << 19),
+        cost_estimate=pl.CostEstimate(
+            flops=4 * size, bytes_accessed=4 * size, transcendentals=slots * clusters
+        ),
+    )(embeddings)
 
 
 def nearest_kernel(place_ref, counts_ref, own_ref, chip_ref, cross_ref, next_ref, out_ref):
@@ -59,8 +96,9 @@
             jnp.concatenate([best[t * groups : (t + 1) * groups] for t in range(slots)], axis=1)
         )
     own_low = member < (member ^ CROSS)
-    out_ref[:groups, 0, :] = jnp.where(own_low, results[0], results[1])
-    out_ref[groups:, 0, :] = jnp.where(own_low, results[1], results[0])
+    low = jnp.where(own_low, results[0], results[1])
+    high = jnp.where(own_low, results[1], results[0])
+    out_ref[...] = jnp.stack([low, high], axis=1)
 
 
 def nearest_of(place, counts, own, chip, cross, nxt):
@@ -69,7 +107,7 @@
     vmem = pl.BlockSpec(memory_space=pltpu.VMEM)
     return pl.pallas_call(
         nearest_kernel,
-        out_shape=jax.ShapeDtypeStruct((2 * groups, 1, rows // groups), jnp.float32),
+        out_shape=jax.ShapeDtypeStruct((groups, 2, rows // groups), jnp.float32),
         in_specs=[pl.BlockSpec(memory_space=pltpu.SMEM)] + [vmem] * 5,
         out_specs=vmem,
         compiler_params=pltpu.CompilerParams(vmem_limit_bytes=32 << 20),
@@ -90,7 +128,7 @@
     assert sorted(ORDER) == list(range(clusters))
     sends = [[c * members + m for c in ORDER] for m in range(members)]
     lows = [m for m in range(members) if m < m ^ CROSS]
-    returns = [[c * members + m for m in (low, low ^ CROSS) for c in ORDER] for low in lows]
+    returns = [[c * members + m for c in ORDER for m in (low, low ^ CROSS)] for low in lows]
 
     def on_device(embeddings, counts):
         group = lax.axis_index("grp")
@@ -98,15 +136,11 @@
         slot_dev = embeddings.shape[1]
         groups = embeddings.shape[2]
         width = embeddings.shape[3]
-        local = embeddings.reshape(slot_dev, groups, width)
-        values = local.astype(jnp.float32)
-        units = (
-            values * lax.rsqrt(jnp.sum(values * values, axis=-1, keepdims=True) + EPS)
-        ).astype(jnp.bfloat16)
+        units = units_by_cluster(embeddings)
         owned = lax.all_to_all(
-            units, ("grp", "mem"), split_axis=1, concat_axis=1, tiled=True, axis_index_groups=sends
+            units, ("grp", "mem"), split_axis=0, concat_axis=0, tiled=True, axis_index_groups=sends
         )
-        rows = owned.reshape(slot_dev * groups, width)
+        rows = jnp.transpose(owned, (1, 0, 2)).reshape(slot_dev * groups, width)
         next_rows = trade(rows, NEXT)
         cross_rows = trade(rows, CROSS)
         chip_rows = both_cores(rows)
@@ -114,9 +148,9 @@
         place = jnp.stack([group, member]).astype(jnp.int32)
         best = nearest_of(place, counts, rows, chip_rows, cross_rows, next_chip_rows)
         back = lax.all_to_all(
-            best, ("grp", "mem"), split_axis=0, concat_axis=0, tiled=True, axis_index_groups=returns
+            best.reshape(2 * groups, 1, slot_dev), ("grp", "mem"), split_axis=0, concat_axis=0, tiled=True, axis_index_groups=returns
         )
-        back = jnp.max(back.reshape(2, groups, slot_dev), axis=0)
+        back = jnp.max(back.reshape(groups, 2, slot_dev), axis=1)
         return back.T.reshape(1, slot_dev, groups)
 
     return on_device

time: 81.3 us -> 80.9 us (level)
  other arithmetic: 1.86 us -> 0.16 us
  Pallas kernels: 1.67 us -> 3.25 us
    pallas_call x1 -> x2, Pallas kernels: 1.67 us -> 3.25 us  [the longest x1 1.68 us: nearest_of(): pl.pallas_call(nearest_kernel, out_shape=jax.ShapeDtypeStruct((groups, 2,...]
    reduce_sum x1 -> x0, other arithmetic: 1.42 us -> none  [on_device(): jnp.sum(values * values, axis=-1, keepdims=True) + EPS]
where the time goes in v8:
time: 80.9 us; the launch traced here: 79.8 us
  blocking collectives  64.1 us (79%)
  waiting for transfers between devices  6.52 us (8%)
  starting transfers between devices  5 us (6%)
  Pallas kernels  3.25 us (4%)
    all_to_all x1, blocking collectives, on_device(): lax.all_to_all(units, ('grp', 'mem'), split_axis=0, concat_axis=0, tiled=...  39.4 us
    all_to_all x1, blocking collectives, on_device(): lax.all_to_all(best.reshape(2 * groups, 1, slot_dev), ('grp', 'mem'), spl...  20 us
    ppermute x2, waiting for transfers between devices, trade(): return lax.ppermute(array, 'mem', [(m, m ^ mask) for m in range(members)])  6.52 us
    ppermute x2, starting transfers between devices, trade(): return lax.ppermute(array, 'mem', [(m, m ^ mask) for m in range(members)])  5 us
    all_gather x2, blocking collectives, both_cores(): return lax.all_gather(array, 'mem', axis=0, axis_index_groups=chips)  4.73 us
    pallas_call x1, Pallas kernels, nearest_of(): pl.pallas_call(nearest_kernel, out_shape=jax.ShapeDtypeStruct((groups, 2,...  1.68 us
  transfers between devices with their start and end apart: 2, of which 1 were waited for; matrix products, arithmetic and copies ran while one was open for 0% of the time, Pallas kernels for 0%

profile of v8, /device:TPU:24, one launch (start us, length us, event | category | flops | bytes accessed | tf_op | source)
XLA Modules:
  0.0 79.8 jit_solution(10716291899113781458)
XLA Ops:
  0.0 1.6 %shard_map.28 = bf16[64,4,768]{2,1,0:T(4,128)(2,1)S(1)} custom-call(bf16[1,4,64,768]{3,2,1,0:T(8,128)(2,1)} %items_ref.1), custom_call_target="tpu_custom_call" | custom-call | flops 786432 | bytes 786432 | tf_op jit(solution)/shard_map/pallas_call | solution.py:47
  1.6 39.4 %all_to_all.10 = bf16[64,4,768]{2,1,0:T(4,128)(2,1)S(1)} all-to-all(bf16[64,4,768]{2,1,0:T(4,128)(2,1)S(1)} %shard_map.28), channel_id=1, replica_groups={{272,264,280,256,144,136,152,128,400,392,408,384,240,232,248,224,304,29..., dimensions={0} | all-to-all | bytes 786432 | tf_op jit(solution)/shard_map/all_to_all | solution.py:140
  41.0 2.1 %collective-permute-start.1 = (bf16[256,768]{1,0:T(8,128)(2,1)S(1)}, bf16[256,768]{1,0:T(8,128)(2,1)S(1)}, u32[]{:S(2)}, u32[]{:S(2)}) collective-permute-start(bf16[256,768]{1,0:T(8,128)(2,1)S(1)} %bitcast.13), channel_id=1, source_target_pairs={{0,6},{1,7},{2,4},{3,5},{4,2},{5,3},{6,0},{7,1},{8,14},{9,15},{10,... | collective-permute-start | bytes 1179656 | tf_op jit(solution)/shard_map/ppermute | solution.py:122
  43.2 0.1 pad_add_fusion.place_ref
  43.2 2.9 %collective-permute-start = (bf16[256,768]{1,0:T(8,128)(2,1)S(1)}, bf16[256,768]{1,0:T(8,128)(2,1)S(1)}, u32[]{:S(2)}, u32[]{:S(2)}) collective-permute-start(bf16[256,768]{1,0:T(8,128)(2,1)S(1)} %bitcast.14), channel_id=1, source_target_pairs={{0,2},{1,3},{2,0},{3,1},{4,6},{5,7},{6,4},{7,5},{8,10},{9,11},{10,... | collective-permute-start | bytes 1179656 | tf_op jit(solution)/shard_map/ppermute | solution.py:122
  46.1 2.4 %all_gather.9.chip_ref = bf16[2,256,768]{2,1,0:T(8,128)(2,1)S(1)} all-gather(bf16[1,256,768]{2,1,0:T(8,128)(2,1)S(1)} %bitcast.15), channel_id=1, replica_groups={{0,1},{2,3},{4,5},{6,7},{8,9},{10,11},{12,13},{14,15},{16,17},{18,19},{..., dimensions={0}, use_global_device_ids=true | all-gather | bytes 1179648 | tf_op jit(solution)/shard_map/all_gather | solution.py:126
  48.5 0.0 copy-start
  48.5 6.5 %collective-permute-done.1 = bf16[256,768]{1,0:T(8,128)(2,1)S(1)} collective-permute-done((bf16[256,768]{1,0:T(8,128)(2,1)S(1)}, bf16[256,768]{1,0:T(8,128)(2,1)S(1)}, u32[]{:S(2)}, u32[]{:S(2)}) %collective-permute-start.1) | collective-permute-done | bytes 393248 | tf_op jit(solution)/shard_map/ppermute | solution.py:122
  55.0 2.4 %all-gather = bf16[512,768]{1,0:T(8,128)(2,1)S(1)} all-gather(bf16[256,768]{1,0:T(8,128)(2,1)S(1)} %collective-permute-done.1), channel_id=2, replica_groups={{0,1},{2,3},{4,5},{6,7},{8,9},{10,11},{12,13},{14,15},{16,17},{18,19},{..., dimensions={0}, use_global_device_ids=true | all-gather | bytes 1179648 | tf_op jit(solution)/shard_map/all_gather | solution.py:126
  57.4 0.0 collective-permute-done.cross_ref
  57.4 0.0 copy-done
  57.4 1.7 %shard_map.29 = f32[64,2,4]{2,1,0:T(2,128)S(1)} custom-call(s32[2]{0:T(128)S(1)} %pad_add_fusion.place_ref, s32[64,64]{1,0:T(8,128)S(1)} %copy-done, bf16[256,768]{1,0:T(8,128)(2,1)S(1)} %bitcast.16, bf16[2,256,768]{2,1,0:T(8,128)(2,1)S(1)} %all_gather.9.chip_ref, bf16[256,768]{1,0:T(8,128)(2,1)S(1)} %collective-permute-done.cross_ref, ...), custom_call_target="tpu_custom_call" | custom-call | flops 805306368 | bytes 1966080 | tf_op jit(solution)/shard_map/pallas_call | solution.py:108
  59.1 20.0 %all_to_all.11 = f32[128,1,4]{2,1,0:T(1,128)S(1)} all-to-all(f32[128,1,4]{2,1,0:T(1,128)S(1)} %bitcast.18), channel_id=1, replica_groups={{272,274,264,266,280,282,256,258,144,146,136,138,152,154,128,130,400,40..., dimensions={0} | all-to-all | bytes 4096 | tf_op jit(solution)/shard_map/all_to_all | solution.py:150
  79.0 0.1 reduce_max.9
  79.1 0.7 copy.11
  (1 shorter events, 0.0 us)
Async XLA Ops:
  41.0 14.0 %collective-permute-start.1 = (bf16[256,768]{1,0:T(8,128)(2,1)S(1)}, bf16[256,768]{1,0:T(8,128)(2,1)S(1)}, u32[]{:S(2)}, u32[]{:S(2)}) collective-permute-start(bf16[256,768]{1,0:T(8,128)(2,1)S(1)} %bitcast.13), channel_id=1, source_target_pairs={{0,6},{1,7},{2,4},{3,5},{4,2},{5,3},{6,0},{7,1},{8,14},{9,15},{10,... | collective-permute-start | bytes 1179656 | tf_op jit(solution)/shard_map/ppermute | solution.py:122
  43.2 14.1 %collective-permute-start = (bf16[256,768]{1,0:T(8,128)(2,1)S(1)}, bf16[256,768]{1,0:T(8,128)(2,1)S(1)}, u32[]{:S(2)}, u32[]{:S(2)}) collective-permute-start(bf16[256,768]{1,0:T(8,128)(2,1)S(1)} %bitcast.14), channel_id=1, source_target_pairs={{0,2},{1,3},{2,0},{3,1},{4,6},{5,7},{6,4},{7,5},{8,10},{9,11},{10,... | collective-permute-start | bytes 1179656 | tf_op jit(solution)/shard_map/ppermute | solution.py:122
  48.5 8.9 %copy-start = (s32[64,64]{1,0:T(8,128)S(1)}, s32[64,64]{1,0:T(8,128)}, u32[]{:S(2)}) copy-start(s32[64,64]{1,0:T(8,128)} %counts_ref.1) | copy-start | bytes 49156

commit v9 on v8

--- a/solution.py
+++ b/solution.py
@@ -76,20 +76,22 @@
 
     keys = []
     for keys_ref, first in ((chip_ref, member & ~CORE), (next_ref, (member ^ NEXT) & ~CORE)):
+        places = []
         for core in range(2):
             start = (first + core) * rows
             slot = (start + lane) // groups
-            keys.append((keys_ref, core, jnp.where(slot < sizes, start + lane, FAR)))
+            places.append(jnp.where(slot < sizes, start + lane, FAR))
+        keys.append((keys_ref, jnp.concatenate(places, axis=1)))
     results = []
     for query_ref, mask in ((own_ref, 0), (cross_ref, CROSS)):
         query_pos = (member ^ mask) * rows + row
         best = jnp.full((rows, LANES), -1.0, jnp.float32)
-        for keys_ref, core, key_pos in keys:
+        for keys_ref, key_pos in keys:
             score = lax.dot_general(
-                query_ref[...], keys_ref[core], (((1,), (1,)), ((), ())), preferred_element_type=jnp.float32
+                query_ref[...], keys_ref[...].reshape(2 * rows, -1), (((1,), (1,)), ((), ())), preferred_element_type=jnp.float32
             )
             score = jnp.where(key_pos < query_pos, score, -1.0)
-            for first in range(0, rows, LANES):
+            for first in range(0, 2 * rows, LANES):
                 best = jnp.maximum(best, score[:, first : first + LANES])
         best = jnp.max(best, axis=1, keepdims=True)
         results.append(

time: 80.9 us -> 80.9 us (level)
  no operation moved by 1% of the time
where the time goes in v9:
time: 80.9 us; the launch traced here: 79.8 us
  blocking collectives  64.1 us (79%)
  waiting for transfers between devices  6.52 us (8%)
  starting transfers between devices  5 us (6%)
  Pallas kernels  3.25 us (4%)
    all_to_all x1, blocking collectives, on_device(): lax.all_to_all(units, ('grp', 'mem'), split_axis=0, concat_axis=0, tiled=...  39.4 us
    all_to_all x1, blocking collectives, on_device(): lax.all_to_all(best.reshape(2 * groups, 1, slot_dev), ('grp', 'mem'), spl...  20 us
    ppermute x2, waiting for transfers between devices, trade(): return lax.ppermute(array, 'mem', [(m, m ^ mask) for m in range(members)])  6.52 us
    ppermute x2, starting transfers between devices, trade(): return lax.ppermute(array, 'mem', [(m, m ^ mask) for m in range(members)])  5 us
    all_gather x2, blocking collectives, both_cores(): return lax.all_gather(array, 'mem', axis=0, axis_index_groups=chips)  4.73 us
    pallas_call x1, Pallas kernels, nearest_of(): pl.pallas_call(nearest_kernel, out_shape=jax.ShapeDtypeStruct((groups, 2,...  1.68 us
  transfers between devices with their start and end apart: 2, of which 1 were waited for; matrix products, arithmetic and copies ran while one was open for 0% of the time, Pallas kernels for 0%

profile of v9, /device:TPU:24, one launch (start us, length us, event | category | flops | bytes accessed | tf_op | source)
XLA Modules:
  0.0 79.8 jit_solution(10716291899113781458)
XLA Ops:
  0.0 1.6 %shard_map.28 = bf16[64,4,768]{2,1,0:T(4,128)(2,1)S(1)} custom-call(bf16[1,4,64,768]{3,2,1,0:T(8,128)(2,1)} %items_ref.1), custom_call_target="tpu_custom_call" | custom-call | flops 786432 | bytes 786432 | tf_op jit(solution)/shard_map/pallas_call | solution.py:47
  1.6 39.4 %all_to_all.10 = bf16[64,4,768]{2,1,0:T(4,128)(2,1)S(1)} all-to-all(bf16[64,4,768]{2,1,0:T(4,128)(2,1)S(1)} %shard_map.28), channel_id=1, replica_groups={{272,264,280,256,144,136,152,128,400,392,408,384,240,232,248,224,304,29..., dimensions={0} | all-to-all | bytes 786432 | tf_op jit(solution)/shard_map/all_to_all | solution.py:142
  41.0 2.1 %collective-permute-start.1 = (bf16[256,768]{1,0:T(8,128)(2,1)S(1)}, bf16[256,768]{1,0:T(8,128)(2,1)S(1)}, u32[]{:S(2)}, u32[]{:S(2)}) collective-permute-start(bf16[256,768]{1,0:T(8,128)(2,1)S(1)} %bitcast.13), channel_id=1, source_target_pairs={{0,6},{1,7},{2,4},{3,5},{4,2},{5,3},{6,0},{7,1},{8,14},{9,15},{10,... | collective-permute-start | bytes 1179656 | tf_op jit(solution)/shard_map/ppermute | solution.py:124
  43.2 0.1 pad_add_fusion.place_ref
  43.2 2.9 %collective-permute-start = (bf16[256,768]{1,0:T(8,128)(2,1)S(1)}, bf16[256,768]{1,0:T(8,128)(2,1)S(1)}, u32[]{:S(2)}, u32[]{:S(2)}) collective-permute-start(bf16[256,768]{1,0:T(8,128)(2,1)S(1)} %bitcast.14), channel_id=1, source_target_pairs={{0,2},{1,3},{2,0},{3,1},{4,6},{5,7},{6,4},{7,5},{8,10},{9,11},{10,... | collective-permute-start | bytes 1179656 | tf_op jit(solution)/shard_map/ppermute | solution.py:124
  46.1 2.4 %all_gather.9.chip_ref = bf16[2,256,768]{2,1,0:T(8,128)(2,1)S(1)} all-gather(bf16[1,256,768]{2,1,0:T(8,128)(2,1)S(1)} %bitcast.15), channel_id=1, replica_groups={{0,1},{2,3},{4,5},{6,7},{8,9},{10,11},{12,13},{14,15},{16,17},{18,19},{..., dimensions={0}, use_global_device_ids=true | all-gather | bytes 1179648 | tf_op jit(solution)/shard_map/all_gather | solution.py:128
  48.5 0.0 copy-start
  48.5 6.5 %collective-permute-done.1 = bf16[256,768]{1,0:T(8,128)(2,1)S(1)} collective-permute-done((bf16[256,768]{1,0:T(8,128)(2,1)S(1)}, bf16[256,768]{1,0:T(8,128)(2,1)S(1)}, u32[]{:S(2)}, u32[]{:S(2)}) %collective-permute-start.1) | collective-permute-done | bytes 393248 | tf_op jit(solution)/shard_map/ppermute | solution.py:124
  55.0 2.4 %all-gather = bf16[512,768]{1,0:T(8,128)(2,1)S(1)} all-gather(bf16[256,768]{1,0:T(8,128)(2,1)S(1)} %collective-permute-done.1), channel_id=2, replica_groups={{0,1},{2,3},{4,5},{6,7},{8,9},{10,11},{12,13},{14,15},{16,17},{18,19},{..., dimensions={0}, use_global_device_ids=true | all-gather | bytes 1179648 | tf_op jit(solution)/shard_map/all_gather | solution.py:128
  57.4 0.0 collective-permute-done.cross_ref
  57.4 0.0 copy-done
  57.4 1.7 %shard_map.29 = f32[64,2,4]{2,1,0:T(2,128)S(1)} custom-call(s32[2]{0:T(128)S(1)} %pad_add_fusion.place_ref, s32[64,64]{1,0:T(8,128)S(1)} %copy-done, bf16[256,768]{1,0:T(8,128)(2,1)S(1)} %bitcast.16, bf16[2,256,768]{2,1,0:T(8,128)(2,1)S(1)} %all_gather.9.chip_ref, bf16[256,768]{1,0:T(8,128)(2,1)S(1)} %collective-permute-done.cross_ref, ...), custom_call_target="tpu_custom_call" | custom-call | flops 805306368 | bytes 1966080 | tf_op jit(solution)/shard_map/pallas_call | solution.py:110
  59.1 20.0 %all_to_all.11 = f32[128,1,4]{2,1,0:T(1,128)S(1)} all-to-all(f32[128,1,4]{2,1,0:T(1,128)S(1)} %bitcast.18), channel_id=1, replica_groups={{272,274,264,266,280,282,256,258,144,146,136,138,152,154,128,130,400,40..., dimensions={0} | all-to-all | bytes 4096 | tf_op jit(solution)/shard_map/all_to_all | solution.py:152
  79.0 0.1 reduce_max.9
  79.1 0.7 copy.11
  (1 shorter events, 0.0 us)
Async XLA Ops:
  41.0 14.0 %collective-permute-start.1 = (bf16[256,768]{1,0:T(8,128)(2,1)S(1)}, bf16[256,768]{1,0:T(8,128)(2,1)S(1)}, u32[]{:S(2)}, u32[]{:S(2)}) collective-permute-start(bf16[256,768]{1,0:T(8,128)(2,1)S(1)} %bitcast.13), channel_id=1, source_target_pairs={{0,6},{1,7},{2,4},{3,5},{4,2},{5,3},{6,0},{7,1},{8,14},{9,15},{10,... | collective-permute-start | bytes 1179656 | tf_op jit(solution)/shard_map/ppermute | solution.py:124
  43.2 14.1 %collective-permute-start = (bf16[256,768]{1,0:T(8,128)(2,1)S(1)}, bf16[256,768]{1,0:T(8,128)(2,1)S(1)}, u32[]{:S(2)}, u32[]{:S(2)}) collective-permute-start(bf16[256,768]{1,0:T(8,128)(2,1)S(1)} %bitcast.14), channel_id=1, source_target_pairs={{0,2},{1,3},{2,0},{3,1},{4,6},{5,7},{6,4},{7,5},{8,10},{9,11},{10,... | collective-permute-start | bytes 1179656 | tf_op jit(solution)/shard_map/ppermute | solution.py:124
  48.5 8.9 %copy-start = (s32[64,64]{1,0:T(8,128)S(1)}, s32[64,64]{1,0:T(8,128)}, u32[]{:S(2)}) copy-start(s32[64,64]{1,0:T(8,128)} %counts_ref.1) | copy-start | bytes 49156
